TPU v7x, 128 devices: a whole 4x4x4 slice. The times are simulated.
128 devices in a mesh: replica: 4 (over y_lo, core), fsdp: 32 (over y_hi, z, x).
Axes of the slice: x: 4, y: 4 (y_hi: 2, y_lo: 2; y = y_hi * 2 + y_lo), z: 4, core: 2. Of those that a mesh axis runs over, the one named last changes fastest.
Arguments:
- inputs: bfloat16 [4, 16384, 1536], P('replica', 'fsdp'), may hold values from -6 to 6
- token_ids: int32 [4, 16384], P('replica', 'fsdp'), may hold values from 0 to 32063, as said below
- upstream: bfloat16 [4, 16384, 6144], P('replica', 'fsdp'), may hold values from -0.119628906 to 0.119628906
- weight: bfloat16 [4, 1536, 6144], P('replica', 'fsdp'), may hold values from -0.15625 to 0.15625
- frag_index: int32 [16], replicated, may hold values from 0 to 15, each once
- global_params: float32 [16, 2097152], P(None, 'fsdp'), may hold values from -6 to 6
- local_params: float32 [4, 16, 2097152], P('replica', None, 'fsdp'), may hold values from -6 to 6
- momentum: float32 [16, 2097152], P(None, 'fsdp'), may hold values from -3 to 3
Outputs:
- weight_grad: bfloat16 [4, 1536, 6144], P('replica', 'fsdp')
- new_global: float32 [2097152], P('fsdp')
- new_momentum: float32 [2097152], P('fsdp')
Inputs may be any that keep to these rules, and one draw needn't show every extreme that they name: `token_ids`: within each aligned block of 512 tokens of a replica, padding (id 0) forms a tail of 0 to 256 tokens; other ids are 1 or more.
All inputs are finite; a program needn't handle non-finite values.
Results may differ from a plain program's by a relative error of at most 0.029.
Values may be sent and summed in bfloat16 or wider, within the bound.
A program may use at most 128 MiB of HBM per device.

v0:
```python
import jax
import jax.numpy as jnp
from jax import lax
from jax.sharding import PartitionSpec as P


def inner_grad(inputs, token_ids, upstream, weight):
    tokens = inputs[0]
    shard = weight[0]
    pre = jnp.dot(
        tokens,
        lax.all_gather(shard, "fsdp", axis=0, tiled=True),
        preferred_element_type=jnp.float32,
    )
    sig = jax.nn.sigmoid(pre)
    deriv = sig * (1.0 + pre * (1.0 - sig))
    keep = (token_ids[0] != 0).astype(jnp.float32)[:, None]
    eff = (keep * upstream[0].astype(jnp.float32) * deriv).astype(jnp.bfloat16)
    summed = lax.psum_scatter(
        lax.dot_general(
            tokens, eff, (((0,), (0,)), ((), ())), preferred_element_type=jnp.float32
        ).astype(jnp.bfloat16),
        "fsdp",
        scatter_dimension=0,
        tiled=True,
    )
    return summed[None]


def outer_update(frag_index, global_params, local_params, momentum):
    fragment = frag_index[0]
    chosen = lax.dynamic_index_in_dim(global_params, fragment, 0, keepdims=False)
    local_now = lax.dynamic_index_in_dim(local_params[0], fragment, 0, keepdims=False)
    moment_now = lax.dynamic_index_in_dim(momentum, fragment, 0, keepdims=False)
    replicas = lax.axis_size("replica")
    difference = chosen - local_now
    delta = lax.psum(difference.astype(jnp.bfloat16), "replica").astype(jnp.float32) / replicas
    new_momentum = 0.9 * moment_now + delta
    new_global = chosen - 0.7 * (delta + 0.9 * new_momentum)
    return (new_global, new_momentum)


def local(inputs, token_ids, upstream, weight, frag_index, global_params, local_params, momentum):
    weight_grad = inner_grad(inputs, token_ids, upstream, weight)
    new_global, new_momentum = outer_update(frag_index, global_params, local_params, momentum)
    return (weight_grad, new_global, new_momentum)


def solution(mesh):
    placed = (
        P("replica", "fsdp", None),
        P("replica", "fsdp"),
        P("replica", "fsdp", None),
        P("replica", "fsdp", None),
        P(),
        P(None, "fsdp"),
        P("replica", None, "fsdp"),
        P(None, "fsdp"),
    )
    return jax.shard_map(
        local,
        mesh=mesh,
        in_specs=placed,
        out_specs=(P("replica", "fsdp", None), P("fsdp"), P("fsdp")),
        check_vma=False,
    )
```

profile of v0, /device:TPU:0, one launch (start us, length us, event | category | flops | bytes accessed | tf_op | source)
XLA Modules:
  0.0 524.4 jit_solution(10218475975486218524)
XLA Ops:
  8.0 0.0 copy-start
  8.0 0.0 all-gather.3.cloned.1.call-start
  8.1 0.7 all-gather.3.cloned.1.call-update
  8.7 0.0 all-reduce.2.cloned.1.call-start
  10.7 1.8 constant_dynamic-slice_fusion.1
  12.5 1.8 constant_dynamic-slice_fusion
  14.3 0.7 subtract_convert_fusion
  15.0 0.0 all-reduce.2.cloned.1.call-update
  15.0 0.0 reduce-scatter.4.cloned.1.call-start
  15.1 0.7 compare_convert_fusion
  15.7 167.6 %all-gather.3.cloned.1.call-done = bf16[1,1536,6144]{2,1,0:T(8,128)(2,1)} async-done(((bf16[1,48,6144]{2,1,0:T(8,128)(2,1)}), bf16[1,1536,6144]{2,1,0:T(8,128)(2,1)}) %all-gather.3.cloned.1.call-update) | async-done | bytes 18874384 | tf_op jit(solution)/shard_map/all_gather | solution.py:12
  183.3 0.0 copy-done
  183.3 28.2 %fusion = bf16[1536,6144]{0,1:T(8,128)(2,1)} fusion(bf16[1,512,6144]{2,1,0:T(8,128)(2,1)} %param.10, f32[512]{0:T(512)S(1)} %bitcast.32, bf16[1,1536,6144]{2,1,0:T(8,128)(2,1)} %all-gather.3.cloned.1.call-done, bf16[1,512,1536]{2,1,0:T(8,128)(2,1)S(1)} %copy-done), kind=kOutput, calls=%fused_computation.1 | convolution fusion | flops 19371393024 | bytes 45615104 | tf_op jit(solution)/shard_map/dot_general | solution.py:20
  211.5 0.0 copy-start.1
  211.5 24.8 %copy.13 = bf16[1536,6144]{1,0:T(8,128)(2,1)} copy(bf16[1536,6144]{0,1:T(8,128)(2,1)} %fusion) | data formatting | bytes 37748736
  236.4 0.0 reduce-scatter.4.cloned.1.call-update
  236.4 1.9 dynamic-slice_multiply_fusion
  238.3 0.0 all-reduce.2.cloned.1.call-done
  238.3 1.8 multiply_subtract_fusion
  240.1 273.8 %reduce-scatter.4.cloned.1.call-done = bf16[48,6144]{1,0:T(8,128)(2,1)} async-done(((bf16[1536,6144]{1,0:T(8,128)(2,1)}), bf16[48,6144]{1,0:T(8,128)(2,1)}) %reduce-scatter.4.cloned.1.call-update) | async-done | bytes 589840
  513.8 1.7 copy.14
  515.6 1.4 copy.12
  516.9 0.0 copy-done.1
Async XLA Ops:
  8.0 175.3 %copy-start = (bf16[1,512,1536]{2,1,0:T(8,128)(2,1)S(1)}, bf16[1,512,1536]{2,1,0:T(8,128)(2,1)}, u32[]{:S(2)}) copy-start(bf16[1,512,1536]{2,1,0:T(8,128)(2,1)} %param.8) | copy-start | bytes 4718596
  8.0 175.3 %all-gather.3.cloned.1.call-start = ((), (), s32[]{:S(2)}) async-start(), calls=%async_computation.2 | async-start | bytes 19464192 | tf_op jit(solution)/shard_map/all_gather | solution.py:12
  8.7 229.5 %all-reduce.2.cloned.1.call-start = ((), (), s32[]{:S(2)}) async-start(), calls=%async_computation.1 | async-start | bytes 262144 | tf_op jit(solution)/shard_map/psum | solution.py:37
  15.0 498.8 %reduce-scatter.4.cloned.1.call-start = ((), (), s32[]{:S(2)}) async-start(), calls=%async_computation.3 | async-start | bytes 19464192
  211.5 305.4 %copy-start.1 = (bf16[1,512,1536]{2,1,0:T(8,128)(2,1)S(1)}, bf16[1,512,1536]{2,1,0:T(8,128)(2,1)}, u32[]{:S(2)}) copy-start(bf16[1,512,1536]{2,1,0:T(8,128)(2,1)} %param.8) | copy-start | bytes 4718596
Sparse Core Ops, SparseCore 0:
  11.9 171.3 all-gather.2
  236.5 277.2 reduce-scatter.3
Sparse Core Ops, SparseCore 1:
  15.1 55.6 all-reduce.1
where the time goes:
time: 525 us; the launch traced here: 524 us
  waiting for transfers between devices  442 us (84%)
  local copies, waits for them, and re-layouts  31.5 us (6%)
  matrix products  28.2 us (5%)
  between operations  17.5 us (3%)
    unnamed x4, waiting for transfers between devices  274 us
    all_gather x1, waiting for transfers between devices, inner_grad(): lax.all_gather(shard, 'fsdp', axis=0, tiled=True)  168 us
    dot_general x1, matrix products, inner_grad(): lax.dot_general(tokens, eff, (((0,), (0,)), ((), ())), preferred_element_...  28.2 us
    unnamed x7, local copies, waits for them, and re-layouts  28 us
  transfers between devices with their start and end apart: 3, of which 2 were waited for; matrix products, arithmetic and copies ran while one was open for 12% of the time, Pallas kernels for 0%

commit v1 on v0

--- a/solution.py
+++ b/solution.py
@@ -1,30 +1,321 @@
+import functools
+
 import jax
 import jax.numpy as jnp
 from jax import lax
+from jax.experimental import pallas as pl
+from jax.experimental.pallas import tpu as pltpu
 from jax.sharding import PartitionSpec as P
 
+MESH = pl.DeviceIdType.MESH
+TOK, DW, FW = 512, 1536, 6144
+ROWS = 48
+HALF = 768
+COLS = 1536
+CHUNKS = ((0, 256), (256, 512), (768, 512), (1280, 256))
+FIRST = ((0, 256), (256, 1280))
+DIST = (1, 3, 2)
+MB = 256
+
+
+def kernel(
+    x_hbm, ids_ref, up_hbm, w_hbm, out_hbm,
+    X, XT, U, W, E, G, RY, RX, T, K,
+    own_sem, a_s, a_r, k_s, k_r, x_s, x_r, u_s, u_r,
+    b_s, b_r, c_s, c_r, d_s, d_r, e_s, e_r, f_s, f_r,
+):
+    core = lax.rem(lax.axis_index("replica"), 2)
+    me = lax.axis_index("fsdp")
+    h, z, x = lax.div(me, 16), lax.rem(lax.div(me, 4), 4), lax.rem(me, 4)
+    p = z + core * (x - z)
+    q = x + core * (z - x)
+
+    def place(hh, pp, qq):
+        return hh * 16 + (pp + core * (qq - pp)) * 4 + (qq + core * (pp - qq))
+
+    def rows(hh, pp, qq):
+        return pl.ds(pl.multiple_of(place(hh, pp, qq) * ROWS, 16), ROWS)
+
+    def ahead(a, d):
+        return lax.rem(a + d, 4)
+
+    def remote(src, dst, send, recv, device):
+        return pltpu.make_async_remote_copy(
+            src_ref=src, dst_ref=dst, send_sem=send, recv_sem=recv,
+            device_id={"fsdp": device}, device_id_type=MESH,
+        )
+
+    sent = []
+
+    def quarter(pp, c0, cw):
+        return pl.ds(pl.multiple_of(pp * COLS + c0, 128), cw)
+
+    barrier = pltpu.get_barrier_semaphore()
+    near = [place(h, ahead(p, d), q) for d in DIST]
+    side = [place(h, p, ahead(q, d)) for d in DIST]
+    over = place(1 - h, p, q)
+    for device in near + side + [over]:
+        pl.semaphore_signal(barrier, inc=1, device_id={"fsdp": device}, device_id_type=MESH)
+    pl.semaphore_wait(barrier, 7)
+
+    own = []
+    weight_in = []
+    for n, (c0, cw) in enumerate(FIRST):
+        place_w = W.at[rows(h, p, q), pl.ds(c0, cw)]
+        copies = []
+        for i, d in enumerate(DIST):
+            copy = remote(
+                w_hbm.at[0, :, quarter(ahead(p, d), c0, cw)], place_w,
+                a_s.at[n, i], a_r.at[n, i], near[i],
+            )
+            copy.start()
+            copies.append(copy)
+        mine = pltpu.make_async_copy(w_hbm.at[0, :, quarter(p, c0, cw)], place_w, own_sem.at[n])
+        mine.start()
+        weight_in.append((mine, copies))
+        sent += copies
+
+    K[p] = jnp.broadcast_to((ids_ref[...] != 0).astype(jnp.float32), (8, TOK))
+    x_in, k_in = [], []
+    for i in range(3):
+        k_in.append(remote(K.at[p], K.at[p], k_s.at[i], k_r.at[i], near[i]))
+        k_in[i].start()
+    for i in range(3):
+        x_in.append(remote(x_hbm.at[0], X.at[p], x_s.at[i], x_r.at[i], near[i]))
+        x_in[i].start()
+    x_own = pltpu.make_async_copy(x_hbm.at[0], X.at[p], own_sem.at[2])
+    x_own.start()
+    u_in = []
+    for n, (c0, cw) in enumerate(CHUNKS):
+        there = U.at[p, :, pl.ds(c0, cw)]
+        copies = []
+        for i, d in enumerate(DIST):
+            copy = remote(
+                up_hbm.at[0, :, quarter(ahead(p, d), c0, cw)], there,
+                u_s.at[n, i], u_r.at[n, i], near[i],
+            )
+            copy.start()
+            copies.append(copy)
+        u_in.append(copies)
+        sent += copies
+    u_own = pltpu.make_async_copy(up_hbm.at[0, :, quarter(p, 0, COLS)], U.at[p], own_sem.at[3])
+    u_own.start()
+    sent += x_in + k_in
+
+    def arrive(copies):
+        for copy in copies:
+            copy.wait_recv()
+
+    side_in = []
+
+    def to_side(n):
+        c0, cw = CHUNKS[n]
+        cols = pl.ds(c0, cw)
+        totals = []
+        for i in range(3):
+            for pp in range(4):
+                part = W.at[rows(h, pp, q), cols]
+                remote(part, part, b_s.at[n, i], b_r.at[n, i], side[i]).start()
+            whole = W.at[pl.ds(0, 4 * ROWS), cols]
+            totals.append(remote(whole, whole, b_s.at[n, i], b_r.at[n, i], side[i]))
+        side_in.append(totals)
+        sent.extend(totals)
+
+    over_in = []
+
+    def to_over(n):
+        arrive(side_in[n])
+        c0, cw = CHUNKS[n]
+        half = W.at[pl.ds(pl.multiple_of(h * HALF, 16), HALF), pl.ds(c0, cw)]
+        copy = remote(half, half, c_s.at[n], c_r.at[n], over)
+        copy.start()
+        over_in.append(copy)
+        sent.append(copy)
+
+    def turn(t):
+        kept = K[t][0:1, :].astype(jnp.bfloat16)
+
+        def step(j, carry):
+            cols = pl.ds(pl.multiple_of(j * 256, 256), 256)
+            XT[t, cols, :] = jnp.transpose(X[t, :, cols]) * kept
+            return carry
+
+        lax.fori_loop(0, DW // 256, step, 0)
+
+    weight_in[0][0].wait()
+    arrive(weight_in[0][1])
+    to_side(0)
+    weight_in[1][0].wait()
+    arrive(weight_in[1][1])
+    for n in range(1, len(CHUNKS)):
+        to_side(n)
+    to_over(0)
+    x_own.wait()
+    turn(p)
+    for n in range(1, len(CHUNKS)):
+        to_over(n)
+    u_own.wait()
+    blocks = [p] + [lax.rem(p - d + 4, 4) for d in DIST]
+    for i in range(3):
+        k_in[i].wait_recv()
+        x_in[i].wait_recv()
+        turn(blocks[i + 1])
+
+    def forward(n, t):
+        c0, cw = CHUNKS[n]
+
+        def step(m, carry):
+            part = pl.ds(pl.multiple_of(m * MB, MB), MB)
+            pre = jnp.dot(X[t, part, :], W[:, c0 : c0 + cw], preferred_element_type=jnp.float32)
+            sig = jax.nn.sigmoid(pre)
+            deriv = sig * (1.0 + pre * (1.0 - sig))
+            eff = U[t, part, c0 : c0 + cw].astype(jnp.float32) * deriv
+            E[t, part, 0:cw] = eff.astype(jnp.bfloat16)
+            return carry
+
+        lax.fori_loop(0, TOK // MB, step, 0)
+
+    def grad(n, half):
+        c0, cw = CHUNKS[n]
+
+        def step(m, carry):
+            part = pl.ds(pl.multiple_of(half * HALF + m * 256, 256), 256)
+            acc = jnp.dot(XT[0, part, :], E[0, :, 0:cw], preferred_element_type=jnp.float32)
+            for t in range(1, 4):
+                acc += jnp.dot(XT[t, part, :], E[t, :, 0:cw], preferred_element_type=jnp.float32)
+            G[part, c0 : c0 + cw] = acc.astype(jnp.bfloat16)
+            return carry
+
+        lax.fori_loop(0, HALF // 256, step, 0)
+
+    back_in = []
+
+    def compute(n):
+        c0, cw = CHUNKS[n]
+        over_in[n].wait_recv()
+        forward(n, blocks[0])
+        for i in range(3):
+            u_in[n][i].wait_recv()
+            forward(n, blocks[i + 1])
+        grad(n, 1 - h)
+        copy = remote(
+            G.at[pl.ds(pl.multiple_of((1 - h) * HALF, 16), HALF), pl.ds(c0, cw)],
+            RY.at[:, pl.ds(c0, cw)], d_s.at[n], d_r.at[n], over,
+        )
+        copy.start()
+        back_in.append(copy)
+        sent.append(copy)
+        grad(n, h)
+
+    sums_in = []
+
+    def reduce_over(n):
+        c0, cw = CHUNKS[n]
+        back_in[n].wait_recv()
+
+        def step(m, carry):
+            here = pl.ds(pl.multiple_of(h * HALF + m * 64, 64), 64)
+            there = pl.ds(pl.multiple_of(m * 64, 64), 64)
+            total = G[here, c0 : c0 + cw].astype(jnp.float32) + RY[there, c0 : c0 + cw].astype(jnp.float32)
+            G[here, c0 : c0 + cw] = total.astype(jnp.bfloat16)
+            return carry
+
+        lax.fori_loop(0, HALF // 64, step, 0)
+        totals = []
+        for i, d in enumerate(DIST):
+            for pp in range(4):
+                remote(
+                    G.at[rows(h, pp, ahead(q, d)), pl.ds(c0, cw)],
+                    RX.at[i, pl.ds(pp * ROWS, ROWS), pl.ds(c0, cw)],
+                    e_s.at[n, i], e_r.at[n, i], side[i],
+                ).start()
+            whole = RX.at[i, :, pl.ds(c0, cw)]
+            totals.append(remote(whole, whole, e_s.at[n, i], e_r.at[n, i], side[i]))
+        sums_in.append(totals)
+        sent.extend(totals)
+
+    last_in = []
+
+    def reduce_side(n):
+        c0, cw = CHUNKS[n]
+        arrive(sums_in[n])
+
+        def step(pp, carry):
+            part = pl.ds(pl.multiple_of(pp * ROWS, 16), ROWS)
+            total = G[rows(h, pp, q), c0 : c0 + cw].astype(jnp.float32)
+            for i in range(3):
+                total += RX[i, part, c0 : c0 + cw].astype(jnp.float32)
+            T[part, c0 : c0 + cw] = total.astype(jnp.bfloat16)
+            return carry
+
+        lax.fori_loop(0, 4, step, 0)
+        there = out_hbm.at[0, :, quarter(p, c0, cw)]
+        copies = []
+        for i, d in enumerate(DIST):
+            part = pl.ds(pl.multiple_of(ahead(p, d) * ROWS, 16), ROWS)
+            copy = remote(T.at[part, pl.ds(c0, cw)], there, f_s.at[n, i], f_r.at[n, i], near[i])
+            copy.start()
+            copies.append(copy)
+        part = pl.ds(pl.multiple_of(p * ROWS, 16), ROWS)
+        mine = pltpu.make_async_copy(T.at[part, pl.ds(c0, cw)], there, own_sem.at[4 + n])
+        mine.start()
+        own.append(mine)
+        last_in.append(copies)
+        sent.extend(copies)
+
+    compute(0)
+    compute(1)
+    compute(2)
+    reduce_over(0)
+    compute(3)
+    reduce_over(1)
+    reduce_side(0)
+    reduce_over(2)
+    reduce_side(1)
+    reduce_over(3)
+    reduce_side(2)
+    reduce_side(3)
+    for copies in last_in:
+        arrive(copies)
+    for mine in own:
+        mine.wait()
+    for copy in sent:
+        copy.wait_send()
+
 
 def inner_grad(inputs, token_ids, upstream, weight):
-    tokens = inputs[0]
-    shard = weight[0]
-    pre = jnp.dot(
-        tokens,
-        lax.all_gather(shard, "fsdp", axis=0, tiled=True),
-        preferred_element_type=jnp.float32,
-    )
-    sig = jax.nn.sigmoid(pre)
-    deriv = sig * (1.0 + pre * (1.0 - sig))
-    keep = (token_ids[0] != 0).astype(jnp.float32)[:, None]
-    eff = (keep * upstream[0].astype(jnp.float32) * deriv).astype(jnp.bfloat16)
-    summed = lax.psum_scatter(
-        lax.dot_general(
-            tokens, eff, (((0,), (0,)), ((), ())), preferred_element_type=jnp.float32
-        ).astype(jnp.bfloat16),
-        "fsdp",
-        scatter_dimension=0,
-        tiled=True,
-    )
-    return summed[None]
+    n = len(CHUNKS)
+    bf16 = jnp.bfloat16
+    sems = [pltpu.SemaphoreType.DMA((4 + n,))]
+    for shape in ((2, 3), (3,), (3,), (n, 3), (n, 3), (n,), (n,), (n, 3), (n, 3)):
+        sems += [pltpu.SemaphoreType.DMA(shape)] * 2
+    hbm = pl.BlockSpec(memory_space=pl.ANY)
+    return pl.pallas_call(
+        kernel,
+        name="inner_grad",
+        out_shape=jax.ShapeDtypeStruct((1, ROWS, FW), bf16),
+        in_specs=[hbm, pl.BlockSpec(memory_space=pltpu.VMEM), hbm, hbm],
+        out_specs=hbm,
+        scratch_shapes=[
+            pltpu.VMEM((4, TOK, DW), bf16),
+            pltpu.VMEM((4, DW, TOK), bf16),
+            pltpu.VMEM((4, TOK, COLS), bf16),
+            pltpu.VMEM((DW, COLS), bf16),
+            pltpu.VMEM((4, TOK, 512), bf16),
+            pltpu.VMEM((DW, COLS), bf16),
+            pltpu.VMEM((HALF, COLS), bf16),
+            pltpu.VMEM((3, 4 * ROWS, COLS), bf16),
+            pltpu.VMEM((4 * ROWS, COLS), bf16),
+            pltpu.VMEM((4, 8, TOK), jnp.float32),
+            *sems,
+        ],
+        compiler_params=pltpu.CompilerParams(
+            collective_id=0, has_side_effects=True, vmem_limit_bytes=52 * 2**20
+        ),
+        cost_estimate=pl.CostEstimate(
+            flops=4 * TOK * DW * FW, bytes_accessed=10 * 2**20, transcendentals=TOK * FW
+        ),
+    )(inputs, token_ids, upstream, weight)
 
 
 def outer_update(frag_index, global_params, local_params, momentum):

time: 525 us -> 162 us (0.31)
  waiting for transfers between devices: 442 us -> 0.04 us
  Pallas kernels: 0 us -> 136 us
  matrix products: 28.2 us -> 0 us
  local copies, waits for them, and re-layouts: 31.5 us -> 6.11 us
    unnamed x4 -> x1, waiting for transfers between devices: 274 us -> 0.02 us
    all_gather x1 -> x0, waiting for transfers between devices: 168 us -> none  [inner_grad(): lax.all_gather(shard, 'fsdp', axis=0, tiled=True)]
    pallas_call x0 -> x1, Pallas kernels: none -> 136 us  [inner_grad(): pl.pallas_call(kernel, name='inner_grad', out_shape=jax.ShapeDtypeStruct(...]
    dot_general x1 -> x0, matrix products: 28.2 us -> none  [inner_grad(): lax.dot_general(tokens, eff, (((0,), (0,)), ((), ())), preferred_element_...]
    unnamed x7 -> x5, local copies, waits for them, and re-layouts: 28 us -> 2.55 us
  transfers between devices with their start and end apart: 3 -> 1, of which waited for: 2 -> 0; matrix products, arithmetic and copies ran while one was open for 12% -> 1% of each run, Pallas kernels for 0% -> 84%
where the time goes in v1:
time: 162 us
  Pallas kernels  136 us (84%)
  between operations  16 us (10%)
  local copies, waits for them, and re-layouts  6.11 us (4%)
  other arithmetic  4.31 us (3%)
    pallas_call x1, Pallas kernels, inner_grad(): pl.pallas_call(kernel, name='inner_grad', out_shape=jax.ShapeDtypeStruct(...  136 us
  transfers between devices with their start and end apart: 1, of which 0 were waited for; matrix products, arithmetic and copies ran while one was open for 1% of the time, Pallas kernels for 84%

profile of v1, /device:TPU:0, one launch (start us, length us, event | category | flops | bytes accessed | tf_op | source)
XLA Modules:
  0.0 162.1 jit_solution(9294742076463071242)
XLA Ops:
  7.2 0.0 all-reduce.2.cloned.1.call-start
  9.1 1.8 %constant_dynamic-slice_fusion = f32[1,1,65536]{2,1,0:T(1,128)S(1)} fusion(f32[1,16,65536]{2,1,0:T(8,128)} %param.14, s32[]{:T(128)S(6)} %select_n.6), kind=kLoop, calls=%fused_computation.5 | loop fusion | bytes 524292 | tf_op jit(solution)/shard_map/jit(dynamic_index_in_dim)/dynamic_slice | solution.py:324
  10.9 1.8 %constant_dynamic-slice_fusion.1 = f32[1,65536]{1,0:T(1,128)S(1)} fusion(f32[16,65536]{1,0:T(8,128)} %param.13, s32[]{:T(128)S(6)} %select_n.6), kind=kLoop, calls=%fused_computation.6 | loop fusion | bytes 524292 | tf_op jit(solution)/shard_map/jit(dynamic_index_in_dim)/dynamic_slice | solution.py:323
  12.7 0.7 subtract_convert_fusion
  13.4 0.0 all-reduce.2.cloned.1.call-update
  13.4 1.9 %dynamic-slice_multiply_fusion = f32[1,65536]{1,0:T(1,128)S(1)} fusion(f32[16,65536]{1,0:T(8,128)} %param.15, s32[]{:T(128)S(6)} %select_n.6), kind=kLoop, calls=%fused_computation.1 | loop fusion | flops 65536 | bytes 524292 | tf_op jit(solution)/shard_map/mul | solution.py:329
  15.3 0.0 copy-start
  15.3 1.1 copy-done
  16.4 0.0 copy-start.1
  16.4 0.7 copy-done.1
  17.0 135.6 %inner_grad.1 = bf16[1,48,6144]{2,1,0:T(8,128)(2,1)S(1)} custom-call(bf16[1,512,1536]{2,1,0:T(8,128)(2,1)} %x_hbm.1, s32[1,512]{1,0:T(1,128)S(1)} %copy-done.1, bf16[1,512,6144]{2,1,0:T(8,128)(2,1)} %up_hbm.1, bf16[1,48,6144]{2,1,0:T(8,128)(2,1)S(1)} %copy-done), custom_call_target="tpu_custom_call" | custom-call | flops 19327352832 | bytes 10485760 | tf_op jit(solution)/shard_map/inner_grad/pallas_call | solution.py:293
  152.7 0.0 all-reduce.2.cloned.1.call-done
  152.7 1.8 %multiply_subtract_fusion = (f32[65536]{0:T(1024)}, f32[65536]{0:T(1024)}) fusion(f32[65536]{0:T(1024)S(1)} %bitcast.6, bf16[65536]{0:T(1024)(128)(2,1)} %all-reduce.2.cloned.1.call-done, f32[65536]{0:T(1024)S(1)} %bitcast.8), kind=kLoop, calls=%fused_computation | loop fusion | flops 458752 | bytes 1179648 | tf_op jit(solution)/shard_map/sub | solution.py:330
  154.4 0.8 copy.13
Async XLA Ops:
  7.2 145.5 %all-reduce.2.cloned.1.call-start = ((), (), s32[]{:S(2)}) async-start(), calls=%async_computation | async-start | bytes 262144 | tf_op jit(solution)/shard_map/psum | solution.py:328
  15.3 1.1 copy-start
  16.4 0.7 copy-start.1
Sparse Core Ops, SparseCore 0:
  13.5 38.8 all-reduce.1

commit v2 on v1

v2 whole, which is shorter than its diff:
```python
import functools

import jax
import jax.numpy as jnp
from jax import lax
from jax.experimental import pallas as pl
from jax.experimental.pallas import tpu as pltpu
from jax.sharding import PartitionSpec as P

MESH = pl.DeviceIdType.MESH
TOK, DW, FW = 512, 1536, 6144
ROWS = 48
HALF = 768
COLS = 1536
WIDE = 256
CHUNKS = tuple((c, WIDE) for c in range(0, COLS, WIDE))
FIRST = ((0, WIDE), (WIDE, COLS - WIDE))
W_OVER_FIRST = (5,)
G_OVER_LAST = (4, 5)
DIST = (1, 3, 2)
MB = 256


def kernel(
    x_hbm, ids_hbm, up_hbm, w_hbm, frag_ref, gp_hbm, lp_hbm, mo_hbm,
    out_hbm, new_global, new_momentum,
    X, XT, U, W, E, G, RY, RX, T, T2, WY, K, IDS,
    GP, LP, MO, CHOSEN, MOMENT, DIFF, DPAIR, PAIR, OTHER, DELTA,
    NEW_G, NEW_M, plan_sem, o_s, o_r, own_sem, a_s, a_r, k_s, k_r, x_s, x_r, u_s, u_r,
    b_s, b_r, c_s, c_r, d_s, d_r, e_s, e_r, f_s, f_r,
    v_s, v_r, g_s, g_r,
):
    ids_in = pltpu.make_async_copy(ids_hbm, IDS, plan_sem.at[3])
    ids_in.start()
    replica = lax.axis_index("replica")
    core, low = lax.rem(replica, 2), lax.div(replica, 2)
    me = lax.axis_index("fsdp")
    h, z, x = lax.div(me, 16), lax.rem(lax.div(me, 4), 4), lax.rem(me, 4)
    p = z + core * (x - z)
    q = x + core * (z - x)

    def place(hh, pp, qq):
        return hh * 16 + (pp + core * (qq - pp)) * 4 + (qq + core * (pp - qq))

    def rows(hh, pp, qq):
        return pl.ds(pl.multiple_of(place(hh, pp, qq) * ROWS, 16), ROWS)

    def ahead(a, d):
        return lax.rem(a + d, 4)

    def remote(src, dst, send, recv, device, axis="fsdp"):
        return pltpu.make_async_remote_copy(
            src_ref=src, dst_ref=dst, send_sem=send, recv_sem=recv,
            device_id={axis: device}, device_id_type=MESH,
        )

    sent = []

    def quarter(pp, c0, cw):
        return pl.ds(pl.multiple_of(pp * COLS + c0, 128), cw)

    barrier = pltpu.get_barrier_semaphore()
    near = [place(h, ahead(p, d), q) for d in DIST]
    side = [place(h, p, ahead(q, d)) for d in DIST]
    over = place(1 - h, p, q)
    for device in near + side + [over]:
        pl.semaphore_signal(barrier, inc=1, device_id={"fsdp": device}, device_id_type=MESH)
    twin, mate = low * 2 + 1 - core, (1 - low) * 2 + core
    for device in (twin, mate):
        pl.semaphore_signal(barrier, inc=1, device_id={"replica": device}, device_id_type=MESH)
    pl.semaphore_wait(barrier, 9)

    own = []
    weight_in = []
    for n, (c0, cw) in enumerate(FIRST):
        place_w = W.at[rows(h, p, q), pl.ds(c0, cw)]
        copies = []
        for i, d in enumerate(DIST):
            copy = remote(
                w_hbm.at[0, :, quarter(ahead(p, d), c0, cw)], place_w,
                a_s.at[n, i], a_r.at[n, i], near[i],
            )
            copy.start()
            copies.append(copy)
        mine = pltpu.make_async_copy(w_hbm.at[0, :, quarter(p, c0, cw)], place_w, own_sem.at[n])
        mine.start()
        weight_in.append((mine, copies))
        sent += copies

    cross_in = {}
    for n in W_OVER_FIRST:
        c0, cw = CHUNKS[n]
        cols = pl.ds(c0, cw)
        for pp in range(4):
            remote(w_hbm.at[0, :, quarter(pp, c0, cw)], WY.at[pp, :, cols], v_s.at[n], v_r.at[n], over).start()
        cross_in[n] = remote(WY.at[:, :, cols], WY.at[:, :, cols], v_s.at[n], v_r.at[n], over)
        sent.append(cross_in[n])

    ids_in.wait()
    K[p] = jnp.broadcast_to((IDS[...] != 0).astype(jnp.float32), (8, TOK))
    x_in, k_in, u_in = [], [], []
    for i in range(2):
        x_in.append(remote(x_hbm.at[0], X.at[p], x_s.at[i], x_r.at[i], near[i]))
        x_in[i].start()
    x_own = pltpu.make_async_copy(x_hbm.at[0], X.at[p], own_sem.at[2])
    x_own.start()
    for i in range(3):
        k_in.append(remote(K.at[p], K.at[p], k_s.at[i], k_r.at[i], near[i]))
        k_in[i].start()

    def send_up(n):
        c0, cw = CHUNKS[n]
        there = U.at[p, :, pl.ds(c0, cw)]
        copies = []
        for i, d in enumerate(DIST):
            copy = remote(
                up_hbm.at[0, :, quarter(ahead(p, d), c0, cw)], there,
                u_s.at[n, i], u_r.at[n, i], near[i],
            )
            copy.start()
            copies.append(copy)
        u_in.append(copies)
        sent.extend(copies)

    send_up(0)
    u_own = pltpu.make_async_copy(up_hbm.at[0, :, quarter(p, 0, COLS)], U.at[p], own_sem.at[3])
    u_own.start()
    blocks = [p] + [lax.rem(p - d + 4, 4) for d in DIST]

    def pass_on():
        for i in range(2):
            x_in[i].wait_recv()
            part = X.at[blocks[i + 1], pl.ds(256 * i, 256)]
            x_in.append(remote(part, part, x_s.at[2 + i], x_r.at[2 + i], near[i]))
            x_in[2 + i].start()
            sent.append(x_in[2 + i])

    sent += x_in + k_in
    plan_in = []
    for i, (source, target) in enumerate(((gp_hbm, GP), (lp_hbm.at[0], LP), (mo_hbm, MO))):
        plan_in.append(pltpu.make_async_copy(source, target, plan_sem.at[i]))
        plan_in[i].start()

    mine_half = pl.ds(pl.multiple_of(core * 256, 16), 256)
    twin_half = pl.ds(pl.multiple_of((1 - core) * 256, 16), 256)
    pair_in = remote(DIFF.at[twin_half], DPAIR, o_s.at[0], o_r.at[0], twin, "replica")
    other_in = remote(PAIR, OTHER, o_s.at[1], o_r.at[1], mate, "replica")
    delta_in = remote(DELTA.at[mine_half], DELTA.at[mine_half], o_s.at[2], o_r.at[2], twin, "replica")
    sent += [pair_in, other_in, delta_in]

    def plan_pick():
        for copy in plan_in:
            copy.wait()
        fragment = frag_ref[0]

        def step(j, carry):
            cols = pl.ds(pl.multiple_of(j * 2048, 2048), 2048)
            part = pl.ds(pl.multiple_of(j * 16, 16), 16)
            chosen = GP[pl.ds(fragment, 1), cols].reshape(16, 128)
            CHOSEN[part, :] = chosen
            MOMENT[part, :] = MO[pl.ds(fragment, 1), cols].reshape(16, 128)
            DIFF[part, :] = (chosen - LP[pl.ds(fragment, 1), cols].reshape(16, 128)).astype(jnp.bfloat16)
            return carry

        lax.fori_loop(0, 32, step, 0)
        pair_in.start()

    def plan_pair():
        pair_in.wait_recv()
        PAIR[...] = (DIFF[mine_half, :].astype(jnp.float32) + DPAIR[...].astype(jnp.float32)).astype(jnp.bfloat16)
        other_in.start()

    def plan_sum():
        other_in.wait_recv()
        total = PAIR[...].astype(jnp.float32) + OTHER[...].astype(jnp.float32)
        DELTA[mine_half, :] = total * 0.25
        delta_in.start()

    def plan_update():
        delta_in.wait_recv()
        delta = DELTA[...]
        moment = 0.9 * MOMENT[...] + delta
        NEW_M[...] = moment
        NEW_G[...] = CHOSEN[...] - 0.7 * (delta + 0.9 * moment)
        for i, (source, target) in enumerate(((NEW_G, new_global), (NEW_M, new_momentum))):
            copy = pltpu.make_async_copy(source, target, plan_sem.at[i])
            copy.start()
            own.append(copy)

    def arrive(copies):
        for copy in copies:
            copy.wait_recv()

    side_in = []

    def planes(n):
        return range(2) if n in W_OVER_FIRST else [h]

    def to_side(n):
        c0, cw = CHUNKS[n]
        cols = pl.ds(c0, cw)
        totals = []
        for i in range(3):
            for hh in planes(n):
                for pp in range(4):
                    part = W.at[rows(hh, pp, q), cols]
                    remote(part, part, b_s.at[n, i], b_r.at[n, i], side[i]).start()
            whole = W.at[pl.ds(0, 4 * ROWS * len(planes(n))), cols]
            totals.append(remote(whole, whole, b_s.at[n, i], b_r.at[n, i], side[i]))
        side_in.append(totals)
        sent.extend(totals)

    over_in = {}

    def to_over(n):
        arrive(side_in[n])
        c0, cw = CHUNKS[n]
        half = W.at[pl.ds(pl.multiple_of(h * HALF, 16), HALF), pl.ds(c0, cw)]
        copy = remote(half, half, c_s.at[n], c_r.at[n], over)
        copy.start()
        over_in[n] = [copy]
        sent.append(copy)

    again_in = {}

    def to_near_again(n):
        cross_in[n].wait_recv()
        c0, cw = CHUNKS[n]
        cols = pl.ds(c0, cw)
        there = W.at[rows(1 - h, p, q), cols]
        copies = []
        for i, d in enumerate(DIST):
            copies.append(remote(WY.at[ahead(p, d), :, cols], there, g_s.at[n, i], g_r.at[n, i], near[i]))
            copies[i].start()
        mine = pltpu.make_async_copy(WY.at[p, :, cols], there, own_sem.at[4 + len(CHUNKS) + n])
        mine.start()
        again_in[n] = (mine, copies)
        sent.extend(copies)

    def to_side_again(n):
        again_in[n][0].wait()
        arrive(again_in[n][1])
        to_side(n)
        over_in[n] = side_in[n]

    def turn(t):
        kept = K[t][0:1, :].astype(jnp.bfloat16)

        def step(j, carry):
            cols = pl.ds(pl.multiple_of(j * 256, 256), 256)
            XT[t, cols, :] = jnp.transpose(X[t, :, cols]) * kept
            return carry

        lax.fori_loop(0, DW // 256, step, 0)

    weight_in[0][0].wait()
    arrive(weight_in[0][1])
    to_side(0)
    weight_in[1][0].wait()
    arrive(weight_in[1][1])
    plain = [n for n in range(len(CHUNKS)) if n not in W_OVER_FIRST]
    for n in plain[1:]:
        to_side(n)
    for n in W_OVER_FIRST:
        to_near_again(n)
    plan_pick()
    to_over(0)
    x_own.wait()
    turn(p)
    to_over(1)
    plan_pair()
    to_over(2)
    pass_on()
    for n in range(1, len(CHUNKS)):
        send_up(n)
    for n in plain[3:]:
        to_over(n)
    for n in W_OVER_FIRST:
        to_side_again(n)
    plan_sum()
    u_own.wait()
    k_in[0].wait_recv()
    turn(blocks[1])
    k_in[1].wait_recv()
    turn(blocks[2])
    k_in[2].wait_recv()
    x_in[2].wait_recv()
    x_in[3].wait_recv()
    turn(blocks[3])
    plan_update()

    def forward(n, t):
        c0, cw = CHUNKS[n]

        def step(m, carry):
            part = pl.ds(pl.multiple_of(m * MB, MB), MB)
            pre = jnp.dot(X[t, part, :], W[:, c0 : c0 + cw], preferred_element_type=jnp.float32)
            sig = jax.nn.sigmoid(pre)
            deriv = sig * (1.0 + pre * (1.0 - sig))
            eff = U[t, part, c0 : c0 + cw].astype(jnp.float32) * deriv
            E[t, part, 0:cw] = eff.astype(jnp.bfloat16)
            return carry

        lax.fori_loop(0, TOK // MB, step, 0)

    def grad(n, half):
        c0, cw = CHUNKS[n]

        def step(m, carry):
            part = pl.ds(pl.multiple_of(half * HALF + m * 256, 256), 256)
            acc = jnp.dot(XT[0, part, :], E[0, :, 0:cw], preferred_element_type=jnp.float32)
            for t in range(1, 4):
                acc += jnp.dot(XT[t, part, :], E[t, :, 0:cw], preferred_element_type=jnp.float32)
            G[part, c0 : c0 + cw] = acc.astype(jnp.bfloat16)
            return carry

        lax.fori_loop(0, HALF // 256, step, 0)

    back_in = {}

    def compute(n):
        c0, cw = CHUNKS[n]
        arrive(over_in[n])
        forward(n, blocks[0])
        for i in range(3):
            u_in[n][i].wait_recv()
            forward(n, blocks[i + 1])
        grad(n, 1 - h)
        if n in G_OVER_LAST:
            grad(n, h)
            add_side(n, range(2))
            return
        copy = remote(
            G.at[pl.ds(pl.multiple_of((1 - h) * HALF, 16), HALF), pl.ds(c0, cw)],
            RY.at[:, pl.ds(c0, cw)], d_s.at[n], d_r.at[n], over,
        )
        copy.start()
        back_in[n] = copy
        sent.append(copy)
        grad(n, h)

    sums_in = {}

    def add_side(n, both):
        c0, cw = CHUNKS[n]
        cols = pl.ds(c0, cw)
        totals = []
        for i, d in enumerate(DIST):
            for j, hh in enumerate(both):
                for pp in range(4):
                    remote(
                        G.at[rows(hh, pp, ahead(q, d)), cols],
                        RX.at[i, pl.ds((4 * j + pp) * ROWS, ROWS), cols],
                        e_s.at[n, i], e_r.at[n, i], side[i],
                    ).start()
            whole = RX.at[i, pl.ds(0, 4 * ROWS * len(both)), cols]
            totals.append(remote(whole, whole, e_s.at[n, i], e_r.at[n, i], side[i]))
        sums_in[n] = totals
        sent.extend(totals)

    def reduce_over(n):
        c0, cw = CHUNKS[n]
        back_in[n].wait_recv()

        def step(m, carry):
            here = pl.ds(pl.multiple_of(h * HALF + m * 64, 64), 64)
            there = pl.ds(pl.multiple_of(m * 64, 64), 64)
            total = G[here, c0 : c0 + cw].astype(jnp.float32) + RY[there, c0 : c0 + cw].astype(jnp.float32)
            G[here, c0 : c0 + cw] = total.astype(jnp.bfloat16)
            return carry

        lax.fori_loop(0, HALF // 64, step, 0)
        add_side(n, [h])

    def side_sum(n, hh, first, target):
        c0, cw = CHUNKS[n]

        def step(pp, carry):
            part = pl.ds(pl.multiple_of(first + pp * ROWS, 16), ROWS)
            total = G[rows(hh, pp, q), c0 : c0 + cw].astype(jnp.float32)
            for i in range(3):
                total += RX[i, part, c0 : c0 + cw].astype(jnp.float32)
            target[pl.ds(pl.multiple_of(pp * ROWS, 16), ROWS), c0 : c0 + cw] = total.astype(jnp.bfloat16)
            return carry

        lax.fori_loop(0, 4, step, 0)

    last_in = []

    def finish(n):
        c0, cw = CHUNKS[n]
        there = out_hbm.at[0, :, quarter(p, c0, cw)]
        copies = []
        for i, d in enumerate(DIST):
            part = pl.ds(pl.multiple_of(ahead(p, d) * ROWS, 16), ROWS)
            copy = remote(T.at[part, pl.ds(c0, cw)], there, f_s.at[n, i], f_r.at[n, i], near[i])
            copy.start()
            copies.append(copy)
        part = pl.ds(pl.multiple_of(p * ROWS, 16), ROWS)
        mine = pltpu.make_async_copy(T.at[part, pl.ds(c0, cw)], there, own_sem.at[4 + n])
        mine.start()
        own.append(mine)
        last_in.append(copies)
        sent.extend(copies)

    def reduce_side(n):
        arrive(sums_in[n])
        if n not in G_OVER_LAST:
            side_sum(n, h, 0, T)
            finish(n)
            return
        c0, cw = CHUNKS[n]
        side_sum(n, 1 - h, (1 - h) * 4 * ROWS, T2)
        cols = pl.ds(c0, cw)
        copy = remote(T2.at[:, cols], RY.at[pl.ds(0, 4 * ROWS), cols], d_s.at[n], d_r.at[n], over)
        copy.start()
        back_in[n] = copy
        sent.append(copy)
        side_sum(n, h, h * 4 * ROWS, T)

    def reduce_last(n):
        c0, cw = CHUNKS[n]
        back_in[n].wait_recv()

        def step(pp, carry):
            part = pl.ds(pl.multiple_of(pp * ROWS, 16), ROWS)
            total = T[part, c0 : c0 + cw].astype(jnp.float32) + RY[part, c0 : c0 + cw].astype(jnp.float32)
            T[part, c0 : c0 + cw] = total.astype(jnp.bfloat16)
            return carry

        lax.fori_loop(0, 4, step, 0)
        finish(n)

    compute(0)
    compute(1)
    compute(2)
    reduce_over(0)
    compute(3)
    reduce_over(1)
    reduce_side(0)
    compute(4)
    reduce_over(2)
    reduce_side(1)
    compute(5)
    reduce_side(4)
    reduce_over(3)
    reduce_side(2)
    reduce_side(5)
    reduce_last(4)
    reduce_side(3)
    reduce_last(5)
    for copies in last_in:
        arrive(copies)
    for mine in own:
        mine.wait()
    for copy in sent:
        copy.wait_send()


def local(inputs, token_ids, upstream, weight, frag_index, global_params, local_params, momentum):
    n = len(CHUNKS)
    bf16, f32 = jnp.bfloat16, jnp.float32
    sems = [pltpu.SemaphoreType.DMA((4,))]
    sems += [pltpu.SemaphoreType.DMA((3,))] * 2
    sems += [pltpu.SemaphoreType.DMA((4 + 2 * n,))]
    for shape in ((2, 3), (3,), (4,), (n, 3), (n, 3), (n,), (n,), (n, 3), (n, 3), (n,), (n, 3)):
        sems += [pltpu.SemaphoreType.DMA(shape)] * 2
    hbm = pl.BlockSpec(memory_space=pltpu.HBM)
    span = global_params.shape[1]
    weight_grad, new_global, new_momentum = pl.pallas_call(
        kernel,
        name="inner_grad_outer_update",
        out_shape=(
            jax.ShapeDtypeStruct((1, ROWS, FW), bf16),
            jax.ShapeDtypeStruct((512, 128), f32),
            jax.ShapeDtypeStruct((512, 128), f32),
        ),
        in_specs=[hbm, hbm, hbm, hbm, pl.BlockSpec(memory_space=pltpu.SMEM), hbm, hbm, hbm],
        out_specs=[pl.BlockSpec(memory_space=pl.ANY)] * 3,
        scratch_shapes=[
            pltpu.VMEM((4, TOK, DW), bf16),
            pltpu.VMEM((4, DW, TOK), bf16),
            pltpu.VMEM((4, TOK, COLS), bf16),
            pltpu.VMEM((DW, COLS), bf16),
            pltpu.VMEM((4, TOK, WIDE), bf16),
            pltpu.VMEM((DW, COLS), bf16),
            pltpu.VMEM((HALF, COLS), bf16),
            pltpu.VMEM((3, 8 * ROWS, COLS), bf16),
            pltpu.VMEM((4 * ROWS, COLS), bf16),
            pltpu.VMEM((4 * ROWS, COLS), bf16),
            pltpu.VMEM((4, ROWS, COLS), bf16),
            pltpu.VMEM((4, 8, TOK), f32),
            pltpu.VMEM((1, TOK), jnp.int32),
            pltpu.VMEM((16, span), f32),
            pltpu.VMEM((16, span), f32),
            pltpu.VMEM((16, span), f32),
            pltpu.VMEM((512, 128), f32),
            pltpu.VMEM((512, 128), f32),
            pltpu.VMEM((512, 128), bf16),
            pltpu.VMEM((256, 128), bf16),
            pltpu.VMEM((256, 128), bf16),
            pltpu.VMEM((256, 128), bf16),
            pltpu.VMEM((512, 128), f32),
            pltpu.VMEM((512, 128), f32),
            pltpu.VMEM((512, 128), f32),
            *sems,
        ],
        compiler_params=pltpu.CompilerParams(
            collective_id=0, has_side_effects=True, vmem_limit_bytes=51 * 2**20
        ),
        cost_estimate=pl.CostEstimate(
            flops=4 * TOK * DW * FW, bytes_accessed=22 * 2**20, transcendentals=TOK * FW
        ),
    )(inputs, token_ids, upstream, weight, frag_index, global_params, local_params, momentum)
    return (weight_grad, new_global.reshape(span), new_momentum.reshape(span))


def solution(mesh):
    placed = (
        P("replica", "fsdp", None),
        P("replica", "fsdp"),
        P("replica", "fsdp", None),
        P("replica", "fsdp", None),
        P(),
        P(None, "fsdp"),
        P("replica", None, "fsdp"),
        P(None, "fsdp"),
    )
    return jax.shard_map(
        local,
        mesh=mesh,
        in_specs=placed,
        out_specs=(P("replica", "fsdp", None), P("fsdp"), P("fsdp")),
        check_vma=False,
    )
```

time: 162 us -> 125 us (0.77)
  Pallas kernels: 136 us -> 119 us
  between operations: 16 us -> 0.65 us
  other arithmetic: 4.31 us -> 0 us
    pallas_call x1, Pallas kernels: 136 us -> 119 us  [local(): pl.pallas_call(kernel, name='inner_grad_outer_update', out_shape=(jax.Sha...]
    dynamic_slice x2 -> x0, local copies, waits for them, and re-layouts: 3.56 us -> none  [the longest x1 1.78 us: outer_update(): lax.dynamic_index_in_dim(global_params, fragment, 0, keepdims=False)]
    unnamed x5 -> x9, local copies, waits for them, and re-layouts: 2.55 us -> 4.65 us
    mul x1 -> x0, other arithmetic: 1.87 us -> none  [outer_update(): new_momentum = 0.9 * moment_now + delta]
    sub x1 -> x0, other arithmetic: 1.75 us -> none  [outer_update(): new_global = chosen - 0.7 * (delta + 0.9 * new_momentum)]
  transfers between devices with their start and end apart: 1 -> 0, of which waited for: 0 -> 0; matrix products, arithmetic and copies ran while one was open for 1% -> 0% of each run, Pallas kernels for 84% -> 0%
where the time goes in v2:
time: 125 us
  Pallas kernels  119 us (95%)
  local copies, waits for them, and re-layouts  4.65 us (4%)
    pallas_call x1, Pallas kernels, local(): pl.pallas_call(kernel, name='inner_grad_outer_update', out_shape=(jax.Sha...  119 us
    unnamed x9, local copies, waits for them, and re-layouts  4.65 us

profile of v2, /device:TPU:0, one launch (start us, length us, event | category | flops | bytes accessed | tf_op | source)
XLA Modules:
  0.0 124.7 jit_solution(15461639102636765953)
XLA Ops:
  0.6 0.0 copy-start
  0.6 1.1 copy-done
  1.7 0.0 copy-start.1
  1.7 0.7 copy-done.1
  2.4 0.0 copy-start.2
  2.4 0.7 copy-done.2
  3.0 119.4 %inner_grad_outer_update.1 = (bf16[1,48,6144]{2,1,0:T(8,128)(2,1)S(1)}, f32[512,128]{1,0:T(8,128)S(1)}, f32[512,128]{1,0:T(8,128)S(1)}) custom-call(bf16[1,512,1536]{2,1,0:T(8,128)(2,1)} %x_hbm.1, s32[1,512]{1,0:T(1,128)S(1)} %copy-done.1, bf16[1,512,6144]{2,1,0:T(8,128)(2,1)} %up_hbm.1, bf16[1,48,6144]{2,1,0:T(8,128)(2,1)S(1)} %copy-done, s32[16]{0:T(128)S(1)} %copy-done.2, ...), custom_call_target="tpu_custom_call" | custom-call | flops 19327352832 | bytes 23068672 | tf_op jit(solution)/shard_map/inner_grad_outer_update/pallas_call | solution.py:470
  122.4 0.8 copy.14
  123.3 0.7 copy.15
  124.0 0.7 copy.16
Async XLA Ops:
  0.6 1.1 copy-start
  1.7 0.7 copy-start.1
  2.4 0.7 copy-start.2

commit v3 on v2

--- a/solution.py
+++ b/solution.py
@@ -18,17 +18,33 @@
 W_OVER_FIRST = (5,)
 G_OVER_LAST = (4, 5)
 DIST = (1, 3, 2)
-MB = 256
+B_DIRECT = (0,)
+EARLY = (
+    ("send_up", 0), ("weight_ready", 0), ("to_side", 0), ("weight_ready", 1), ("to_side", 1), ("to_side", 2),
+    ("to_near_again", 5), ("pick",), ("pass_side", 1), ("to_over", 0), ("to_side", 3), ("pass_side", 2),
+    ("to_over", 1), ("to_side", 4), ("turn_own",), ("pass_side", 3), ("to_over", 2), ("pair",), ("pass_side", 4),
+    ("pass_on", 0), ("pass_on", 1), ("send_up", 1), ("pass_up", 0), ("send_up", 2), ("to_over", 3),
+    ("to_side_again", 5), ("to_over", 4), ("sum",), ("up_own",), ("turn_near", 0), ("turn_near", 1),
+    ("pass_up", 1), ("send_up", 3), ("pass_side_again", 5), ("update",), ("turn_far",),
+)
+LATE = (
+    ("compute", 0), ("pass_up", 2), ("send_up", 4), ("compute", 1), ("pass_up", 3), ("send_up", 5), ("compute", 2),
+    ("pass_up", 4), ("over", 0), ("compute", 3), ("pass_up", 5), ("over", 1), ("side", 0), ("compute", 4),
+    ("compute", 5), ("over", 2), ("far_plane", 4), ("side", 1), ("drain",), ("far_plane", 5), ("own_plane", 4), ("over", 3),
+    ("side", 2), ("own_plane", 5), ("last", 4), ("last", 5), ("side", 3),
+)
+MB = 512
+GM = 384
 
 
 def kernel(
     x_hbm, ids_hbm, up_hbm, w_hbm, frag_ref, gp_hbm, lp_hbm, mo_hbm,
     out_hbm, new_global, new_momentum,
-    X, XT, U, W, E, G, RY, RX, T, T2, WY, K, IDS,
+    X, XT, U, W, E, G, RY, RX, T, T2, WY, UR, K, IDS,
     GP, LP, MO, CHOSEN, MOMENT, DIFF, DPAIR, PAIR, OTHER, DELTA,
     NEW_G, NEW_M, plan_sem, o_s, o_r, own_sem, a_s, a_r, k_s, k_r, x_s, x_r, u_s, u_r,
     b_s, b_r, c_s, c_r, d_s, d_r, e_s, e_r, f_s, f_r,
-    v_s, v_r, g_s, g_r,
+    v_s, v_r, g_s, g_r, r_s, r_r,
 ):
     ids_in = pltpu.make_async_copy(ids_hbm, IDS, plan_sem.at[3])
     ids_in.start()
@@ -54,7 +70,15 @@
             device_id={axis: device}, device_id_type=MESH,
         )
 
-    sent = []
+    own, sent = [], []
+
+    def drain():
+        for mine in own:
+            mine.wait()
+        for copy in sent:
+            copy.wait_send()
+        own.clear()
+        sent.clear()
 
     def quarter(pp, c0, cw):
         return pl.ds(pl.multiple_of(pp * COLS + c0, 128), cw)
@@ -70,7 +94,6 @@
         pl.semaphore_signal(barrier, inc=1, device_id={"replica": device}, device_id_type=MESH)
     pl.semaphore_wait(barrier, 9)
 
-    own = []
     weight_in = []
     for n, (c0, cw) in enumerate(FIRST):
         place_w = W.at[rows(h, p, q), pl.ds(c0, cw)]
@@ -98,7 +121,7 @@
 
     ids_in.wait()
     K[p] = jnp.broadcast_to((IDS[...] != 0).astype(jnp.float32), (8, TOK))
-    x_in, k_in, u_in = [], [], []
+    x_in, k_in, u_in = [], [], {}
     for i in range(2):
         x_in.append(remote(x_hbm.at[0], X.at[p], x_s.at[i], x_r.at[i], near[i]))
         x_in[i].start()
@@ -108,32 +131,45 @@
         k_in.append(remote(K.at[p], K.at[p], k_s.at[i], k_r.at[i], near[i]))
         k_in[i].start()
 
+    relay_in = {}
+
     def send_up(n):
         c0, cw = CHUNKS[n]
         there = U.at[p, :, pl.ds(c0, cw)]
-        copies = []
-        for i, d in enumerate(DIST):
+        u_in[n], relay_in[n] = [], []
+        far = quarter(ahead(p, 2), c0, cw)
+        for i in range(2):
             copy = remote(
-                up_hbm.at[0, :, quarter(ahead(p, d), c0, cw)], there,
+                up_hbm.at[0, :, quarter(ahead(p, DIST[i]), c0, cw)], there,
                 u_s.at[n, i], u_r.at[n, i], near[i],
             )
+            half = remote(up_hbm.at[0, pl.ds(256 * i, 256), far], UR.at[i, n], r_s.at[n, i], r_r.at[n, i], near[i])
             copy.start()
-            copies.append(copy)
-        u_in.append(copies)
-        sent.extend(copies)
-
-    send_up(0)
+            half.start()
+            u_in[n].append(copy)
+            relay_in[n].append(half)
+        sent.extend(u_in[n] + relay_in[n])
+
+    def pass_up(n):
+        c0, cw = CHUNKS[n]
+        for i in range(2):
+            relay_in[n][i].wait_recv()
+            there = U.at[blocks[i + 1], pl.ds(256 * i, 256), pl.ds(c0, cw)]
+            copy = remote(UR.at[i, n], there, u_s.at[n, 2 + i], u_r.at[n, 2 + i], near[i])
+            copy.start()
+            u_in[n].append(copy)
+            sent.append(copy)
+
     u_own = pltpu.make_async_copy(up_hbm.at[0, :, quarter(p, 0, COLS)], U.at[p], own_sem.at[3])
     u_own.start()
     blocks = [p] + [lax.rem(p - d + 4, 4) for d in DIST]
 
-    def pass_on():
-        for i in range(2):
-            x_in[i].wait_recv()
-            part = X.at[blocks[i + 1], pl.ds(256 * i, 256)]
-            x_in.append(remote(part, part, x_s.at[2 + i], x_r.at[2 + i], near[i]))
-            x_in[2 + i].start()
-            sent.append(x_in[2 + i])
+    def pass_on(i):
+        x_in[i].wait_recv()
+        part = X.at[blocks[i + 1], pl.ds(256 * i, 256)]
+        x_in.append(remote(part, part, x_s.at[2 + i], x_r.at[2 + i], near[i]))
+        x_in[2 + i].start()
+        sent.append(x_in[2 + i])
 
     sent += x_in + k_in
     plan_in = []
@@ -191,7 +227,7 @@
         for copy in copies:
             copy.wait_recv()
 
-    side_in = []
+    side_in = {}
 
     def planes(n):
         return range(2) if n in W_OVER_FIRST else [h]
@@ -200,20 +236,34 @@
         c0, cw = CHUNKS[n]
         cols = pl.ds(c0, cw)
         totals = []
-        for i in range(3):
+        for i in range(3 if n in B_DIRECT else 2):
             for hh in planes(n):
                 for pp in range(4):
                     part = W.at[rows(hh, pp, q), cols]
                     remote(part, part, b_s.at[n, i], b_r.at[n, i], side[i]).start()
             whole = W.at[pl.ds(0, 4 * ROWS * len(planes(n))), cols]
             totals.append(remote(whole, whole, b_s.at[n, i], b_r.at[n, i], side[i]))
-        side_in.append(totals)
+        side_in[n] = totals
         sent.extend(totals)
 
+    def pass_side(n):
+        c0, cw = CHUNKS[n]
+        cols = pl.ds(c0, cw)
+        for i in range(2):
+            side_in[n][i].wait_recv()
+            for hh in planes(n):
+                for pp in (2 * i, 2 * i + 1):
+                    part = W.at[rows(hh, pp, lax.rem(q - DIST[i] + 4, 4)), cols]
+                    remote(part, part, b_s.at[n, 2 + i], b_r.at[n, 2 + i], side[i]).start()
+            whole = W.at[pl.ds(0, 2 * ROWS * len(planes(n))), cols]
+            total = remote(whole, whole, b_s.at[n, 2 + i], b_r.at[n, 2 + i], side[i])
+            side_in[n].append(total)
+            sent.append(total)
+
     over_in = {}
 
     def to_over(n):
-        arrive(side_in[n])
+        arrive(side_in[n] if n in B_DIRECT else side_in[n][2:])
         c0, cw = CHUNKS[n]
         half = W.at[pl.ds(pl.multiple_of(h * HALF, 16), HALF), pl.ds(c0, cw)]
         copy = remote(half, half, c_s.at[n], c_r.at[n], over)
@@ -241,136 +291,137 @@
         again_in[n][0].wait()
         arrive(again_in[n][1])
         to_side(n)
-        over_in[n] = side_in[n]
+
+    def pass_side_again(n):
+        pass_side(n)
+        over_in[n] = side_in[n][2:]
 
     def turn(t):
         kept = K[t][0:1, :].astype(jnp.bfloat16)
 
         def step(j, carry):
             cols = pl.ds(pl.multiple_of(j * 256, 256), 256)
-            XT[t, cols, :] = jnp.transpose(X[t, :, cols]) * kept
+            XT[cols, pl.ds(pl.multiple_of(t * TOK, TOK), TOK)] = jnp.transpose(X[t, :, cols]) * kept
             return carry
 
         lax.fori_loop(0, DW // 256, step, 0)
 
-    weight_in[0][0].wait()
-    arrive(weight_in[0][1])
-    to_side(0)
-    weight_in[1][0].wait()
-    arrive(weight_in[1][1])
-    plain = [n for n in range(len(CHUNKS)) if n not in W_OVER_FIRST]
-    for n in plain[1:]:
-        to_side(n)
-    for n in W_OVER_FIRST:
-        to_near_again(n)
-    plan_pick()
-    to_over(0)
-    x_own.wait()
-    turn(p)
-    to_over(1)
-    plan_pair()
-    to_over(2)
-    pass_on()
-    for n in range(1, len(CHUNKS)):
-        send_up(n)
-    for n in plain[3:]:
-        to_over(n)
-    for n in W_OVER_FIRST:
-        to_side_again(n)
-    plan_sum()
-    u_own.wait()
-    k_in[0].wait_recv()
-    turn(blocks[1])
-    k_in[1].wait_recv()
-    turn(blocks[2])
-    k_in[2].wait_recv()
-    x_in[2].wait_recv()
-    x_in[3].wait_recv()
-    turn(blocks[3])
-    plan_update()
-
-    def forward(n, t):
-        c0, cw = CHUNKS[n]
-
-        def step(m, carry):
+    def weight_ready(n):
+        weight_in[n][0].wait()
+        arrive(weight_in[n][1])
+
+    def turn_own():
+        x_own.wait()
+        turn(p)
+
+    def turn_near(i):
+        k_in[i].wait_recv()
+        turn(blocks[i + 1])
+
+    def turn_far():
+        k_in[2].wait_recv()
+        x_in[2].wait_recv()
+        x_in[3].wait_recv()
+        turn(blocks[3])
+
+    early = {
+        "weight_ready": weight_ready, "to_side": to_side, "to_near_again": to_near_again, "to_over": to_over,
+        "to_side_again": to_side_again, "send_up": send_up, "pass_on": pass_on, "pass_up": pass_up, "pass_side": pass_side, "pass_side_again": pass_side_again, "turn_own": turn_own,
+        "turn_near": turn_near, "turn_far": turn_far, "pick": plan_pick, "pair": plan_pair, "sum": plan_sum,
+        "update": plan_update, "up_own": u_own.wait,
+    }
+    for name, *which in EARLY:
+        early[name](*which)
+
+    def forward(n):
+        c0, cw = CHUNKS[n]
+        steps = TOK // MB
+
+        def step(k, carry):
+            b, m = lax.div(k, steps), lax.rem(k, steps)
+            for i in range(2):
+                pl.when(k == (i + 1) * steps)(u_in[n][i].wait_recv)
+            pl.when(k == 3 * steps)(lambda: arrive(u_in[n][2:]))
+            t = lax.rem(p - (b + lax.div(b, 2) - 2 * lax.div(b, 3)) + 4, 4)
             part = pl.ds(pl.multiple_of(m * MB, MB), MB)
             pre = jnp.dot(X[t, part, :], W[:, c0 : c0 + cw], preferred_element_type=jnp.float32)
-            sig = jax.nn.sigmoid(pre)
+            sig = 0.5 + 0.5 * jnp.tanh(0.5 * pre)
             deriv = sig * (1.0 + pre * (1.0 - sig))
             eff = U[t, part, c0 : c0 + cw].astype(jnp.float32) * deriv
-            E[t, part, 0:cw] = eff.astype(jnp.bfloat16)
-            return carry
-
-        lax.fori_loop(0, TOK // MB, step, 0)
-
-    def grad(n, half):
-        c0, cw = CHUNKS[n]
+            E[pl.ds(pl.multiple_of(t * TOK + m * MB, MB), MB), 0:cw] = eff.astype(jnp.bfloat16)
+            return carry
+
+        lax.fori_loop(0, 4 * steps, step, 0)
+
+    back_in = {}
+
+    def compute(n):
+        c0, cw = CHUNKS[n]
+        arrive(over_in[n])
+        forward(n)
+        steps = HALF // GM
+        if n in G_OVER_LAST:
+            prepare_side(n, 0)
+            prepare_side(n, 1)
+        else:
+            back_in[n] = remote(
+                G.at[pl.ds(pl.multiple_of((1 - h) * HALF, 16), HALF), pl.ds(c0, cw)],
+                RY.at[:, pl.ds(c0, cw)], d_s.at[n], d_r.at[n], over,
+            )
+            sent.append(back_in[n])
+
+        def step(k, carry):
+            own_half = lax.div(k, steps)
+            half = (1 - h) * (1 - own_half) + h * own_half
+            part = pl.ds(pl.multiple_of(half * HALF + lax.rem(k, steps) * GM, GM), GM)
+            acc = jnp.dot(XT[part, :], E[:, 0:cw], preferred_element_type=jnp.float32)
+            G[part, c0 : c0 + cw] = acc.astype(jnp.bfloat16)
+            if n in G_OVER_LAST:
+                pl.when(k == steps - 1)(lambda: start_side(n, 1 - h, 0))
+            else:
+                pl.when(k == steps - 1)(back_in[n].start)
+            return carry
+
+        lax.fori_loop(0, 2 * steps, step, 0)
+        if n in G_OVER_LAST:
+            start_side(n, h, 1)
+
+    sums_in = {}
+
+    def start_side(n, hh, j):
+        c0, cw = CHUNKS[n]
+        cols = pl.ds(c0, cw)
+        for i, d in enumerate(DIST):
+            for pp in range(4):
+                remote(
+                    G.at[rows(hh, pp, ahead(q, d)), cols],
+                    RX.at[i, pl.ds((4 * j + pp) * ROWS, ROWS), cols],
+                    e_s.at[n, 3 * j + i], e_r.at[n, 3 * j + i], side[i],
+                ).start()
+
+    def prepare_side(n, j):
+        c0, cw = CHUNKS[n]
+        totals = []
+        for i in range(3):
+            whole = RX.at[i, pl.ds(4 * ROWS * j, 4 * ROWS), pl.ds(c0, cw)]
+            totals.append(remote(whole, whole, e_s.at[n, 3 * j + i], e_r.at[n, 3 * j + i], side[i]))
+        sums_in[n, j] = totals
+        sent.extend(totals)
+
+    def reduce_over(n):
+        c0, cw = CHUNKS[n]
+        back_in[n].wait_recv()
 
         def step(m, carry):
-            part = pl.ds(pl.multiple_of(half * HALF + m * 256, 256), 256)
-            acc = jnp.dot(XT[0, part, :], E[0, :, 0:cw], preferred_element_type=jnp.float32)
-            for t in range(1, 4):
-                acc += jnp.dot(XT[t, part, :], E[t, :, 0:cw], preferred_element_type=jnp.float32)
-            G[part, c0 : c0 + cw] = acc.astype(jnp.bfloat16)
-            return carry
-
-        lax.fori_loop(0, HALF // 256, step, 0)
-
-    back_in = {}
-
-    def compute(n):
-        c0, cw = CHUNKS[n]
-        arrive(over_in[n])
-        forward(n, blocks[0])
-        for i in range(3):
-            u_in[n][i].wait_recv()
-            forward(n, blocks[i + 1])
-        grad(n, 1 - h)
-        if n in G_OVER_LAST:
-            grad(n, h)
-            add_side(n, range(2))
-            return
-        copy = remote(
-            G.at[pl.ds(pl.multiple_of((1 - h) * HALF, 16), HALF), pl.ds(c0, cw)],
-            RY.at[:, pl.ds(c0, cw)], d_s.at[n], d_r.at[n], over,
-        )
-        copy.start()
-        back_in[n] = copy
-        sent.append(copy)
-        grad(n, h)
-
-    sums_in = {}
-
-    def add_side(n, both):
-        c0, cw = CHUNKS[n]
-        cols = pl.ds(c0, cw)
-        totals = []
-        for i, d in enumerate(DIST):
-            for j, hh in enumerate(both):
-                for pp in range(4):
-                    remote(
-                        G.at[rows(hh, pp, ahead(q, d)), cols],
-                        RX.at[i, pl.ds((4 * j + pp) * ROWS, ROWS), cols],
-                        e_s.at[n, i], e_r.at[n, i], side[i],
-                    ).start()
-            whole = RX.at[i, pl.ds(0, 4 * ROWS * len(both)), cols]
-            totals.append(remote(whole, whole, e_s.at[n, i], e_r.at[n, i], side[i]))
-        sums_in[n] = totals
-        sent.extend(totals)
-
-    def reduce_over(n):
-        c0, cw = CHUNKS[n]
-        back_in[n].wait_recv()
-
-        def step(m, carry):
-            here = pl.ds(pl.multiple_of(h * HALF + m * 64, 64), 64)
-            there = pl.ds(pl.multiple_of(m * 64, 64), 64)
+            here = pl.ds(pl.multiple_of(h * HALF + m * 256, 256), 256)
+            there = pl.ds(pl.multiple_of(m * 256, 256), 256)
             total = G[here, c0 : c0 + cw].astype(jnp.float32) + RY[there, c0 : c0 + cw].astype(jnp.float32)
             G[here, c0 : c0 + cw] = total.astype(jnp.bfloat16)
             return carry
 
-        lax.fori_loop(0, HALF // 64, step, 0)
-        add_side(n, [h])
+        lax.fori_loop(0, HALF // 256, step, 0)
+        prepare_side(n, 0)
+        start_side(n, h, 0)
 
     def side_sum(n, hh, first, target):
         c0, cw = CHUNKS[n]
@@ -404,19 +455,23 @@
         sent.extend(copies)
 
     def reduce_side(n):
-        arrive(sums_in[n])
-        if n not in G_OVER_LAST:
-            side_sum(n, h, 0, T)
-            finish(n)
-            return
-        c0, cw = CHUNKS[n]
-        side_sum(n, 1 - h, (1 - h) * 4 * ROWS, T2)
+        arrive(sums_in[n, 0])
+        side_sum(n, h, 0, T)
+        finish(n)
+
+    def reduce_far_plane(n):
+        arrive(sums_in[n, 0])
+        side_sum(n, 1 - h, 0, T2)
+        c0, cw = CHUNKS[n]
         cols = pl.ds(c0, cw)
         copy = remote(T2.at[:, cols], RY.at[pl.ds(0, 4 * ROWS), cols], d_s.at[n], d_r.at[n], over)
         copy.start()
         back_in[n] = copy
         sent.append(copy)
-        side_sum(n, h, h * 4 * ROWS, T)
+
+    def reduce_own_plane(n):
+        arrive(sums_in[n, 1])
+        side_sum(n, h, 4 * ROWS, T)
 
     def reduce_last(n):
         c0, cw = CHUNKS[n]
@@ -431,30 +486,14 @@
         lax.fori_loop(0, 4, step, 0)
         finish(n)
 
-    compute(0)
-    compute(1)
-    compute(2)
-    reduce_over(0)
-    compute(3)
-    reduce_over(1)
-    reduce_side(0)
-    compute(4)
-    reduce_over(2)
-    reduce_side(1)
-    compute(5)
-    reduce_side(4)
-    reduce_over(3)
-    reduce_side(2)
-    reduce_side(5)
-    reduce_last(4)
-    reduce_side(3)
-    reduce_last(5)
+    late = {"compute": compute, "over": reduce_over, "side": reduce_side, "last": reduce_last}
+    late.update({"drain": drain, "far_plane": reduce_far_plane, "own_plane": reduce_own_plane})
+    late.update(early)
+    for name, *which in LATE:
+        late[name](*which)
     for copies in last_in:
         arrive(copies)
-    for mine in own:
-        mine.wait()
-    for copy in sent:
-        copy.wait_send()
+    drain()
 
 
 def local(inputs, token_ids, upstream, weight, frag_index, global_params, local_params, momentum):
@@ -463,7 +502,7 @@
     sems = [pltpu.SemaphoreType.DMA((4,))]
     sems += [pltpu.SemaphoreType.DMA((3,))] * 2
     sems += [pltpu.SemaphoreType.DMA((4 + 2 * n,))]
-    for shape in ((2, 3), (3,), (4,), (n, 3), (n, 3), (n,), (n,), (n, 3), (n, 3), (n,), (n, 3)):
+    for shape in ((2, 3), (3,), (4,), (n, 4), (n, 4), (n,), (n,), (n, 6), (n, 3), (n,), (n, 3), (n, 2)):
         sems += [pltpu.SemaphoreType.DMA(shape)] * 2
     hbm = pl.BlockSpec(memory_space=pltpu.HBM)
     span = global_params.shape[1]
@@ -479,16 +518,17 @@
         out_specs=[pl.BlockSpec(memory_space=pl.ANY)] * 3,
         scratch_shapes=[
             pltpu.VMEM((4, TOK, DW), bf16),
-            pltpu.VMEM((4, DW, TOK), bf16),
+            pltpu.VMEM((DW, 4 * TOK), bf16),
             pltpu.VMEM((4, TOK, COLS), bf16),
             pltpu.VMEM((DW, COLS), bf16),
-            pltpu.VMEM((4, TOK, WIDE), bf16),
+            pltpu.VMEM((4 * TOK, WIDE), bf16),
             pltpu.VMEM((DW, COLS), bf16),
             pltpu.VMEM((HALF, COLS), bf16),
             pltpu.VMEM((3, 8 * ROWS, COLS), bf16),
             pltpu.VMEM((4 * ROWS, COLS), bf16),
             pltpu.VMEM((4 * ROWS, COLS), bf16),
             pltpu.VMEM((4, ROWS, COLS), bf16),
+            pltpu.VMEM((2, n, 256, WIDE), bf16),
             pltpu.VMEM((4, 8, TOK), f32),
             pltpu.VMEM((1, TOK), jnp.int32),
             pltpu.VMEM((16, span), f32),
@@ -506,7 +546,7 @@
             *sems,
         ],
         compiler_params=pltpu.CompilerParams(
-            collective_id=0, has_side_effects=True, vmem_limit_bytes=51 * 2**20
+            collective_id=0, has_side_effects=True, vmem_limit_bytes=53 * 2**20
         ),
         cost_estimate=pl.CostEstimate(
             flops=4 * TOK * DW * FW, bytes_accessed=22 * 2**20, transcendentals=TOK * FW

time: 125 us -> 121 us (0.968)
  Pallas kernels: 119 us -> 115 us
    pallas_call x1, Pallas kernels: 119 us -> 115 us  [local(): pl.pallas_call(kernel, name='inner_grad_outer_update', out_shape=(jax.Sha...]
    unnamed x9 -> x7, local copies, waits for them, and re-layouts: 4.65 us -> 4.69 us
where the time goes in v3:
time: 121 us
  Pallas kernels  115 us (95%)
  local copies, waits for them, and re-layouts  4.69 us (4%)
    pallas_call x1, Pallas kernels, local(): pl.pallas_call(kernel, name='inner_grad_outer_update', out_shape=(jax.Sha...  115 us
    unnamed x7, local copies, waits for them, and re-layouts  4.69 us

profile of v3, /device:TPU:0, one launch (start us, length us, event | category | flops | bytes accessed | tf_op | source)
XLA Modules:
  0.0 120.7 jit_solution(14332823021991229460)
XLA Ops:
  0.6 0.0 copy-start
  0.6 0.7 copy-done
  1.3 0.0 copy-start.1
  1.3 0.7 copy-done.1
  2.0 115.4 %inner_grad_outer_update.1 = (bf16[1,48,6144]{2,1,0:T(8,128)(2,1)}, f32[512,128]{1,0:T(8,128)S(1)}, f32[512,128]{1,0:T(8,128)S(1)}) custom-call(bf16[1,512,1536]{2,1,0:T(8,128)(2,1)} %x_hbm.1, s32[1,512]{1,0:T(1,128)S(1)} %copy-done, bf16[1,512,6144]{2,1,0:T(8,128)(2,1)} %up_hbm.1, bf16[1,48,6144]{2,1,0:T(8,128)(2,1)} %w_hbm.1, s32[16]{0:T(128)S(1)} %copy-done.1, ...), custom_call_target="tpu_custom_call" | custom-call | flops 19327352832 | bytes 23068672 | tf_op jit(solution)/shard_map/inner_grad_outer_update/pallas_call | solution.py:509
  117.3 1.9 %copy.14 = bf16[1,48,6144]{2,1,0:T(8,128)(2,1)} copy(bf16[1,48,6144]{2,1,0:T(8,128)(2,1)} %get-tuple-element.12) | data formatting | bytes 1179648
  119.3 0.7 copy.15
  120.0 0.7 copy.16
Async XLA Ops:
  0.6 0.7 copy-start
  1.3 0.7 copy-start.1

commit v4 on v3

--- a/solution.py
+++ b/solution.py
@@ -23,14 +23,15 @@
     ("send_up", 0), ("weight_ready", 0), ("to_side", 0), ("weight_ready", 1), ("to_side", 1), ("to_side", 2),
     ("to_near_again", 5), ("pick",), ("pass_side", 1), ("to_over", 0), ("to_side", 3), ("pass_side", 2),
     ("to_over", 1), ("to_side", 4), ("turn_own",), ("pass_side", 3), ("to_over", 2), ("pair",), ("pass_side", 4),
-    ("pass_on", 0), ("pass_on", 1), ("send_up", 1), ("pass_up", 0), ("send_up", 2), ("to_over", 3),
-    ("to_side_again", 5), ("to_over", 4), ("sum",), ("up_own",), ("turn_near", 0), ("turn_near", 1),
-    ("pass_up", 1), ("send_up", 3), ("pass_side_again", 5), ("update",), ("turn_far",),
+    ("up_own",), ("forward", 0, 1), ("pass_on", 0), ("pass_on", 1), ("to_over", 3), ("pass_up", 0), ("send_up", 1),
+    ("send_up", 2), ("to_side_again", 5), ("to_over", 4), ("turn_near", 0), ("turn_near", 1), ("forward", 0, 3),
+    ("forward", 1, 1), ("turn_far",), ("pass_up", 1), ("send_up", 3),
 )
 LATE = (
-    ("compute", 0), ("pass_up", 2), ("send_up", 4), ("compute", 1), ("pass_up", 3), ("send_up", 5), ("compute", 2),
+    ("compute", 0), ("sum",), ("pass_side_again", 5), ("pass_up", 2), ("send_up", 4), ("compute", 1), ("update",),
+    ("pass_up", 3), ("send_up", 5), ("compute", 2),
     ("pass_up", 4), ("over", 0), ("compute", 3), ("pass_up", 5), ("over", 1), ("side", 0), ("compute", 4),
-    ("compute", 5), ("over", 2), ("far_plane", 4), ("side", 1), ("drain",), ("far_plane", 5), ("own_plane", 4), ("over", 3),
+    ("compute", 5), ("over", 2), ("far_plane", 4), ("side", 1), ("far_plane", 5), ("own_plane", 4), ("over", 3),
     ("side", 2), ("own_plane", 5), ("last", 4), ("last", 5), ("side", 3),
 )
 MB = 512
@@ -40,11 +41,11 @@
 def kernel(
     x_hbm, ids_hbm, up_hbm, w_hbm, frag_ref, gp_hbm, lp_hbm, mo_hbm,
     out_hbm, new_global, new_momentum,
-    X, XT, U, W, E, G, RY, RX, T, T2, WY, UR, K, IDS,
+    X, XT, U, W, G, RY, RX, T, T2, WY, UR, K, IDS,
     GP, LP, MO, CHOSEN, MOMENT, DIFF, DPAIR, PAIR, OTHER, DELTA,
     NEW_G, NEW_M, plan_sem, o_s, o_r, own_sem, a_s, a_r, k_s, k_r, x_s, x_r, u_s, u_r,
     b_s, b_r, c_s, c_r, d_s, d_r, e_s, e_r, f_s, f_r,
-    v_s, v_r, g_s, g_r, r_s, r_r,
+    v_s, v_r, g_s, g_r, r_r,
 ):
     ids_in = pltpu.make_async_copy(ids_hbm, IDS, plan_sem.at[3])
     ids_in.start()
@@ -60,6 +61,9 @@
 
     def rows(hh, pp, qq):
         return pl.ds(pl.multiple_of(place(hh, pp, qq) * ROWS, 16), ROWS)
+
+    def dist(i):
+        return 1 + 2 * i - 3 * lax.div(i, 2)
 
     def ahead(a, d):
         return lax.rem(a + d, 4)
@@ -135,32 +139,32 @@
 
     def send_up(n):
         c0, cw = CHUNKS[n]
-        there = U.at[p, :, pl.ds(c0, cw)]
+        there = U.at[pl.ds(pl.multiple_of(p * TOK, TOK), TOK), pl.ds(c0, cw)]
         u_in[n], relay_in[n] = [], []
         far = quarter(ahead(p, 2), c0, cw)
         for i in range(2):
             copy = remote(
                 up_hbm.at[0, :, quarter(ahead(p, DIST[i]), c0, cw)], there,
-                u_s.at[n, i], u_r.at[n, i], near[i],
+                u_s, u_r.at[n, i], near[i],
             )
-            half = remote(up_hbm.at[0, pl.ds(256 * i, 256), far], UR.at[i, n], r_s.at[n, i], r_r.at[n, i], near[i])
+            half = remote(up_hbm.at[0, pl.ds(256 * i, 256), far], UR.at[i, n], u_s, r_r.at[n, i], near[i])
             copy.start()
             half.start()
             u_in[n].append(copy)
             relay_in[n].append(half)
-        sent.extend(u_in[n] + relay_in[n])
 
     def pass_up(n):
         c0, cw = CHUNKS[n]
         for i in range(2):
             relay_in[n][i].wait_recv()
-            there = U.at[blocks[i + 1], pl.ds(256 * i, 256), pl.ds(c0, cw)]
-            copy = remote(UR.at[i, n], there, u_s.at[n, 2 + i], u_r.at[n, 2 + i], near[i])
+            there = U.at[pl.ds(pl.multiple_of(blocks[i + 1] * TOK + 256 * i, 256), 256), pl.ds(c0, cw)]
+            copy = remote(UR.at[i, n], there, u_s, u_r.at[n, 2 + i], near[i])
             copy.start()
             u_in[n].append(copy)
-            sent.append(copy)
-
-    u_own = pltpu.make_async_copy(up_hbm.at[0, :, quarter(p, 0, COLS)], U.at[p], own_sem.at[3])
+
+    u_own = pltpu.make_async_copy(
+        up_hbm.at[0, :, quarter(p, 0, COLS)], U.at[pl.ds(pl.multiple_of(p * TOK, TOK), TOK)], own_sem.at[3]
+    )
     u_own.start()
     blocks = [p] + [lax.rem(p - d + 4, 4) for d in DIST]
 
@@ -235,30 +239,35 @@
     def to_side(n):
         c0, cw = CHUNKS[n]
         cols = pl.ds(c0, cw)
-        totals = []
-        for i in range(3 if n in B_DIRECT else 2):
-            for hh in planes(n):
-                for pp in range(4):
-                    part = W.at[rows(hh, pp, q), cols]
-                    remote(part, part, b_s.at[n, i], b_r.at[n, i], side[i]).start()
-            whole = W.at[pl.ds(0, 4 * ROWS * len(planes(n))), cols]
-            totals.append(remote(whole, whole, b_s.at[n, i], b_r.at[n, i], side[i]))
-        side_in[n] = totals
-        sent.extend(totals)
+        both = len(planes(n))
+        count = 3 if n in B_DIRECT else 2
+
+        def step(k, carry):
+            i, hh, pp = lax.div(k, 4 * both), lax.rem(lax.div(k, 4), both), lax.rem(k, 4)
+            part = W.at[rows(hh if both == 2 else h, pp, q), cols]
+            remote(part, part, b_s, b_r.at[n, i], place(h, p, ahead(q, dist(i)))).start()
+            return carry
+
+        lax.fori_loop(0, 4 * both * count, step, 0)
+        whole = W.at[pl.ds(0, 4 * ROWS * both), cols]
+        side_in[n] = [remote(whole, whole, b_s, b_r.at[n, i], side[i]) for i in range(count)]
 
     def pass_side(n):
         c0, cw = CHUNKS[n]
         cols = pl.ds(c0, cw)
+        both = len(planes(n))
+        whole = W.at[pl.ds(0, 2 * ROWS * both), cols]
         for i in range(2):
             side_in[n][i].wait_recv()
-            for hh in planes(n):
-                for pp in (2 * i, 2 * i + 1):
-                    part = W.at[rows(hh, pp, lax.rem(q - DIST[i] + 4, 4)), cols]
-                    remote(part, part, b_s.at[n, 2 + i], b_r.at[n, 2 + i], side[i]).start()
-            whole = W.at[pl.ds(0, 2 * ROWS * len(planes(n))), cols]
-            total = remote(whole, whole, b_s.at[n, 2 + i], b_r.at[n, 2 + i], side[i])
-            side_in[n].append(total)
-            sent.append(total)
+
+            def step(k, carry, i=i):
+                hh, pp = lax.div(k, 2), 2 * i + lax.rem(k, 2)
+                part = W.at[rows(hh if both == 2 else h, pp, lax.rem(q - DIST[i] + 4, 4)), cols]
+                remote(part, part, b_s, b_r.at[n, 2 + i], side[i]).start()
+                return carry
+
+            lax.fori_loop(0, 2 * both, step, 0)
+            side_in[n].append(remote(whole, whole, b_s, b_r.at[n, 2 + i], side[i]))
 
     over_in = {}
 
@@ -324,41 +333,51 @@
         x_in[3].wait_recv()
         turn(blocks[3])
 
+    def effect(t, m, c):
+        part = pl.ds(pl.multiple_of(m * MB, MB), MB)
+        cols = pl.ds(pl.multiple_of(c * WIDE, WIDE), WIDE)
+        pre = jnp.dot(X[t, part, :], W[:, cols], preferred_element_type=jnp.float32)
+        sig = 0.5 + 0.5 * jnp.tanh(0.5 * pre)
+        deriv = sig * (1.0 + pre * (1.0 - sig))
+        here = pl.ds(pl.multiple_of(t * TOK + m * MB, MB), MB)
+        U[here, cols] = (U[here, cols].astype(jnp.float32) * deriv).astype(jnp.bfloat16)
+
+    steps_in = TOK // MB
+    done = {n: 0 for n in range(len(CHUNKS))}
+
+    def forward(n, last):
+        first = done[n]
+        done[n] = last
+        if first == 0:
+            arrive(over_in[n])
+
+        def step(k, carry):
+            b, m = lax.div(k, steps_in), lax.rem(k, steps_in)
+            for i in range(2):
+                if first <= i + 1 < last:
+                    pl.when(k == (i + 1) * steps_in)(u_in[n][i].wait_recv)
+            if last == 4:
+                pl.when(k == 3 * steps_in)(lambda: arrive(u_in[n][2:]))
+            t = lax.rem(p - (b + lax.div(b, 2) - 2 * lax.div(b, 3)) + 4, 4)
+            effect(t, m, n)
+            return carry
+
+        lax.fori_loop(first * steps_in, last * steps_in, step, 0)
+
     early = {
         "weight_ready": weight_ready, "to_side": to_side, "to_near_again": to_near_again, "to_over": to_over,
         "to_side_again": to_side_again, "send_up": send_up, "pass_on": pass_on, "pass_up": pass_up, "pass_side": pass_side, "pass_side_again": pass_side_again, "turn_own": turn_own,
         "turn_near": turn_near, "turn_far": turn_far, "pick": plan_pick, "pair": plan_pair, "sum": plan_sum,
-        "update": plan_update, "up_own": u_own.wait,
+        "update": plan_update, "up_own": u_own.wait, "forward": forward,
     }
     for name, *which in EARLY:
         early[name](*which)
 
-    def forward(n):
-        c0, cw = CHUNKS[n]
-        steps = TOK // MB
-
-        def step(k, carry):
-            b, m = lax.div(k, steps), lax.rem(k, steps)
-            for i in range(2):
-                pl.when(k == (i + 1) * steps)(u_in[n][i].wait_recv)
-            pl.when(k == 3 * steps)(lambda: arrive(u_in[n][2:]))
-            t = lax.rem(p - (b + lax.div(b, 2) - 2 * lax.div(b, 3)) + 4, 4)
-            part = pl.ds(pl.multiple_of(m * MB, MB), MB)
-            pre = jnp.dot(X[t, part, :], W[:, c0 : c0 + cw], preferred_element_type=jnp.float32)
-            sig = 0.5 + 0.5 * jnp.tanh(0.5 * pre)
-            deriv = sig * (1.0 + pre * (1.0 - sig))
-            eff = U[t, part, c0 : c0 + cw].astype(jnp.float32) * deriv
-            E[pl.ds(pl.multiple_of(t * TOK + m * MB, MB), MB), 0:cw] = eff.astype(jnp.bfloat16)
-            return carry
-
-        lax.fori_loop(0, 4 * steps, step, 0)
-
     back_in = {}
 
     def compute(n):
         c0, cw = CHUNKS[n]
-        arrive(over_in[n])
-        forward(n)
+        forward(n, 4)
         steps = HALF // GM
         if n in G_OVER_LAST:
             prepare_side(n, 0)
@@ -374,7 +393,7 @@
             own_half = lax.div(k, steps)
             half = (1 - h) * (1 - own_half) + h * own_half
             part = pl.ds(pl.multiple_of(half * HALF + lax.rem(k, steps) * GM, GM), GM)
-            acc = jnp.dot(XT[part, :], E[:, 0:cw], preferred_element_type=jnp.float32)
+            acc = jnp.dot(XT[part, :], U[:, c0 : c0 + cw], preferred_element_type=jnp.float32)
             G[part, c0 : c0 + cw] = acc.astype(jnp.bfloat16)
             if n in G_OVER_LAST:
                 pl.when(k == steps - 1)(lambda: start_side(n, 1 - h, 0))
@@ -391,22 +410,23 @@
     def start_side(n, hh, j):
         c0, cw = CHUNKS[n]
         cols = pl.ds(c0, cw)
-        for i, d in enumerate(DIST):
-            for pp in range(4):
-                remote(
-                    G.at[rows(hh, pp, ahead(q, d)), cols],
-                    RX.at[i, pl.ds((4 * j + pp) * ROWS, ROWS), cols],
-                    e_s.at[n, 3 * j + i], e_r.at[n, 3 * j + i], side[i],
-                ).start()
+
+        def step(k, carry):
+            i, pp = lax.div(k, 4), lax.rem(k, 4)
+            to = ahead(q, dist(i))
+            remote(
+                G.at[rows(hh, pp, to), cols],
+                RX.at[i, pl.ds(pl.multiple_of((4 * j + pp) * ROWS, 16), ROWS), cols],
+                e_s, e_r.at[n, 3 * j + i], place(h, p, to),
+            ).start()
+            return carry
+
+        lax.fori_loop(0, 12, step, 0)
 
     def prepare_side(n, j):
         c0, cw = CHUNKS[n]
-        totals = []
-        for i in range(3):
-            whole = RX.at[i, pl.ds(4 * ROWS * j, 4 * ROWS), pl.ds(c0, cw)]
-            totals.append(remote(whole, whole, e_s.at[n, 3 * j + i], e_r.at[n, 3 * j + i], side[i]))
-        sums_in[n, j] = totals
-        sent.extend(totals)
+        whole = RX.at[0, pl.ds(4 * ROWS * j, 4 * ROWS), pl.ds(c0, cw)]
+        sums_in[n, j] = [remote(whole, whole, e_s, e_r.at[n, 3 * j + i], side[i]) for i in range(3)]
 
     def reduce_over(n):
         c0, cw = CHUNKS[n]
@@ -436,23 +456,21 @@
 
         lax.fori_loop(0, 4, step, 0)
 
-    last_in = []
-
     def finish(n):
         c0, cw = CHUNKS[n]
         there = out_hbm.at[0, :, quarter(p, c0, cw)]
-        copies = []
-        for i, d in enumerate(DIST):
-            part = pl.ds(pl.multiple_of(ahead(p, d) * ROWS, 16), ROWS)
-            copy = remote(T.at[part, pl.ds(c0, cw)], there, f_s.at[n, i], f_r.at[n, i], near[i])
-            copy.start()
-            copies.append(copy)
+
+        def step(i, carry):
+            to = ahead(p, dist(i))
+            part = pl.ds(pl.multiple_of(to * ROWS, 16), ROWS)
+            remote(T.at[part, pl.ds(c0, cw)], there, f_s, f_r, place(h, to, q)).start()
+            return carry
+
+        lax.fori_loop(0, 3, step, 0)
         part = pl.ds(pl.multiple_of(p * ROWS, 16), ROWS)
         mine = pltpu.make_async_copy(T.at[part, pl.ds(c0, cw)], there, own_sem.at[4 + n])
         mine.start()
         own.append(mine)
-        last_in.append(copies)
-        sent.extend(copies)
 
     def reduce_side(n):
         arrive(sums_in[n, 0])
@@ -491,19 +509,29 @@
     late.update(early)
     for name, *which in LATE:
         late[name](*which)
-    for copies in last_in:
-        arrive(copies)
+    total = T.at[pl.ds(0, 3 * len(CHUNKS) * ROWS * WIDE // COLS)]
+    all_f = remote(total, total, f_s, f_r, near[0])
+    all_f.wait_recv()
+    units = 12 * ROWS * WIDE // COLS
+    total = W.at[pl.ds(0, units * (len(CHUNKS) + len(W_OVER_FIRST)))]
+    all_b = remote(total, total, b_s, f_r, near[0])
+    total = G.at[pl.ds(0, units * (len(CHUNKS) + len(G_OVER_LAST)))]
+    all_e = remote(total, total, e_s, f_r, near[0])
+    sent.extend([all_f, all_b, all_e, remote(U, U, u_s, f_r, near[0])])
     drain()
 
 
 def local(inputs, token_ids, upstream, weight, frag_index, global_params, local_params, momentum):
     n = len(CHUNKS)
     bf16, f32 = jnp.bfloat16, jnp.float32
-    sems = [pltpu.SemaphoreType.DMA((4,))]
-    sems += [pltpu.SemaphoreType.DMA((3,))] * 2
-    sems += [pltpu.SemaphoreType.DMA((4 + 2 * n,))]
-    for shape in ((2, 3), (3,), (4,), (n, 4), (n, 4), (n,), (n,), (n, 6), (n, 3), (n,), (n, 3), (n, 2)):
-        sems += [pltpu.SemaphoreType.DMA(shape)] * 2
+    dma = pltpu.SemaphoreType.DMA
+    sems = [dma((4,)), dma((3,)), dma((3,)), dma((4 + 2 * n,))]
+    for send, receive in (
+        ((2, 3), (2, 3)), ((3,), (3,)), ((4,), (4,)), ((), (n, 4)), ((), (n, 4)), ((n,), (n,)), ((n,), (n,)),
+        ((), (n, 6)), ((), ()), ((n,), (n,)), ((n, 3), (n, 3)),
+    ):
+        sems += [dma(send), dma(receive)]
+    sems.append(dma((n, 2)))
     hbm = pl.BlockSpec(memory_space=pltpu.HBM)
     span = global_params.shape[1]
     weight_grad, new_global, new_momentum = pl.pallas_call(
@@ -519,9 +547,8 @@
         scratch_shapes=[
             pltpu.VMEM((4, TOK, DW), bf16),
             pltpu.VMEM((DW, 4 * TOK), bf16),
-            pltpu.VMEM((4, TOK, COLS), bf16),
+            pltpu.VMEM((4 * TOK, COLS), bf16),
             pltpu.VMEM((DW, COLS), bf16),
-            pltpu.VMEM((4 * TOK, WIDE), bf16),
             pltpu.VMEM((DW, COLS), bf16),
             pltpu.VMEM((HALF, COLS), bf16),
             pltpu.VMEM((3, 8 * ROWS, COLS), bf16),

time: 121 us -> 120 us (level)
  no operation moved by 1% of the time
where the time goes in v4:
time: 120 us
  Pallas kernels  114 us (95%)
  local copies, waits for them, and re-layouts  4.69 us (4%)
    pallas_call x1, Pallas kernels, local(): pl.pallas_call(kernel, name='inner_grad_outer_update', out_shape=(jax.Sha...  114 us
    unnamed x7, local copies, waits for them, and re-layouts  4.69 us

profile of v4, /device:TPU:0, one launch (start us, length us, event | category | flops | bytes accessed | tf_op | source)
XLA Modules:
  0.0 119.6 jit_solution(1948907074496911840)
XLA Ops:
  0.6 0.0 copy-start
  0.6 0.7 copy-done
  1.3 0.0 copy-start.1
  1.3 0.7 copy-done.1
  2.0 114.2 %inner_grad_outer_update.1 = (bf16[1,48,6144]{2,1,0:T(8,128)(2,1)}, f32[512,128]{1,0:T(8,128)S(1)}, f32[512,128]{1,0:T(8,128)S(1)}) custom-call(bf16[1,512,1536]{2,1,0:T(8,128)(2,1)} %x_hbm.1, s32[1,512]{1,0:T(1,128)S(1)} %copy-done, bf16[1,512,6144]{2,1,0:T(8,128)(2,1)} %up_hbm.1, bf16[1,48,6144]{2,1,0:T(8,128)(2,1)} %w_hbm.1, s32[16]{0:T(128)S(1)} %copy-done.1, ...), custom_call_target="tpu_custom_call" | custom-call | flops 19327352832 | bytes 23068672 | tf_op jit(solution)/shard_map/inner_grad_outer_update/pallas_call | solution.py:537
  116.2 1.9 %copy.14 = bf16[1,48,6144]{2,1,0:T(8,128)(2,1)} copy(bf16[1,48,6144]{2,1,0:T(8,128)(2,1)} %get-tuple-element.12) | data formatting | bytes 1179648
  118.1 0.7 copy.15
  118.9 0.7 copy.16
Async XLA Ops:
  0.6 0.7 copy-start
  1.3 0.7 copy-start.1

commit v5 on v4

--- a/solution.py
+++ b/solution.py
@@ -41,7 +41,7 @@
 def kernel(
     x_hbm, ids_hbm, up_hbm, w_hbm, frag_ref, gp_hbm, lp_hbm, mo_hbm,
     out_hbm, new_global, new_momentum,
-    X, XT, U, W, G, RY, RX, T, T2, WY, UR, K, IDS,
+    X, XT, U, W, G, RY, RX, T, T2, TY, WY, UR, K, IDS,
     GP, LP, MO, CHOSEN, MOMENT, DIFF, DPAIR, PAIR, OTHER, DELTA,
     NEW_G, NEW_M, plan_sem, o_s, o_r, own_sem, a_s, a_r, k_s, k_r, x_s, x_r, u_s, u_r,
     b_s, b_r, c_s, c_r, d_s, d_r, e_s, e_r, f_s, f_r,
@@ -384,8 +384,7 @@
             prepare_side(n, 1)
         else:
             back_in[n] = remote(
-                G.at[pl.ds(pl.multiple_of((1 - h) * HALF, 16), HALF), pl.ds(c0, cw)],
-                RY.at[:, pl.ds(c0, cw)], d_s.at[n], d_r.at[n], over,
+                G.at[1 - h, :, :, :, pl.ds(c0, cw)], RY.at[:, :, :, pl.ds(c0, cw)], d_s.at[n], d_r.at[n], over,
             )
             sent.append(back_in[n])
 
@@ -394,7 +393,8 @@
             half = (1 - h) * (1 - own_half) + h * own_half
             part = pl.ds(pl.multiple_of(half * HALF + lax.rem(k, steps) * GM, GM), GM)
             acc = jnp.dot(XT[part, :], U[:, c0 : c0 + cw], preferred_element_type=jnp.float32)
-            G[part, c0 : c0 + cw] = acc.astype(jnp.bfloat16)
+            planes_z = pl.ds(lax.rem(k, steps) * (GM // 192), GM // 192)
+            G[half, planes_z, :, :, c0 : c0 + cw] = acc.astype(jnp.bfloat16).reshape(GM // 192, 4, ROWS, cw)
             if n in G_OVER_LAST:
                 pl.when(k == steps - 1)(lambda: start_side(n, 1 - h, 0))
             else:
@@ -411,21 +411,26 @@
         c0, cw = CHUNKS[n]
         cols = pl.ds(c0, cw)
 
-        def step(k, carry):
-            i, pp = lax.div(k, 4), lax.rem(k, 4)
+        def step(i, carry):
             to = ahead(q, dist(i))
-            remote(
-                G.at[rows(hh, pp, to), cols],
-                RX.at[i, pl.ds(pl.multiple_of((4 * j + pp) * ROWS, 16), ROWS), cols],
-                e_s, e_r.at[n, 3 * j + i], place(h, p, to),
-            ).start()
-            return carry
-
-        lax.fori_loop(0, 12, step, 0)
+            there = RX.at[i, pl.ds(4 * j, 4), :, cols]
+            device = place(h, p, to)
+
+            @pl.when(core == 0)
+            def _():
+                remote(G.at[hh, :, to, :, cols], there, e_s, e_r.at[n, 3 * j + i], device).start()
+
+            @pl.when(core == 1)
+            def _():
+                remote(G.at[hh, to, :, :, cols], there, e_s, e_r.at[n, 3 * j + i], device).start()
+
+            return carry
+
+        lax.fori_loop(0, 3, step, 0)
 
     def prepare_side(n, j):
         c0, cw = CHUNKS[n]
-        whole = RX.at[0, pl.ds(4 * ROWS * j, 4 * ROWS), pl.ds(c0, cw)]
+        whole = RX.at[0, pl.ds(4 * j, 4), :, pl.ds(c0, cw)]
         sums_in[n, j] = [remote(whole, whole, e_s, e_r.at[n, 3 * j + i], side[i]) for i in range(3)]
 
     def reduce_over(n):
@@ -433,13 +438,11 @@
         back_in[n].wait_recv()
 
         def step(m, carry):
-            here = pl.ds(pl.multiple_of(h * HALF + m * 256, 256), 256)
-            there = pl.ds(pl.multiple_of(m * 256, 256), 256)
-            total = G[here, c0 : c0 + cw].astype(jnp.float32) + RY[there, c0 : c0 + cw].astype(jnp.float32)
-            G[here, c0 : c0 + cw] = total.astype(jnp.bfloat16)
-            return carry
-
-        lax.fori_loop(0, HALF // 256, step, 0)
+            total = G[h, m, :, :, c0 : c0 + cw].astype(jnp.float32) + RY[m, :, :, c0 : c0 + cw].astype(jnp.float32)
+            G[h, m, :, :, c0 : c0 + cw] = total.astype(jnp.bfloat16)
+            return carry
+
+        lax.fori_loop(0, 4, step, 0)
         prepare_side(n, 0)
         start_side(n, h, 0)
 
@@ -447,10 +450,10 @@
         c0, cw = CHUNKS[n]
 
         def step(pp, carry):
-            part = pl.ds(pl.multiple_of(first + pp * ROWS, 16), ROWS)
-            total = G[rows(hh, pp, q), c0 : c0 + cw].astype(jnp.float32)
+            zz, xx = pp + core * (q - pp), q + core * (pp - q)
+            total = G[hh, zz, xx, :, c0 : c0 + cw].astype(jnp.float32)
             for i in range(3):
-                total += RX[i, part, c0 : c0 + cw].astype(jnp.float32)
+                total += RX[i, first + pp, :, c0 : c0 + cw].astype(jnp.float32)
             target[pl.ds(pl.multiple_of(pp * ROWS, 16), ROWS), c0 : c0 + cw] = total.astype(jnp.bfloat16)
             return carry
 
@@ -482,14 +485,14 @@
         side_sum(n, 1 - h, 0, T2)
         c0, cw = CHUNKS[n]
         cols = pl.ds(c0, cw)
-        copy = remote(T2.at[:, cols], RY.at[pl.ds(0, 4 * ROWS), cols], d_s.at[n], d_r.at[n], over)
+        copy = remote(T2.at[:, cols], TY.at[:, cols], d_s.at[n], d_r.at[n], over)
         copy.start()
         back_in[n] = copy
         sent.append(copy)
 
     def reduce_own_plane(n):
         arrive(sums_in[n, 1])
-        side_sum(n, h, 4 * ROWS, T)
+        side_sum(n, h, 4, T)
 
     def reduce_last(n):
         c0, cw = CHUNKS[n]
@@ -497,7 +500,7 @@
 
         def step(pp, carry):
             part = pl.ds(pl.multiple_of(pp * ROWS, 16), ROWS)
-            total = T[part, c0 : c0 + cw].astype(jnp.float32) + RY[part, c0 : c0 + cw].astype(jnp.float32)
+            total = T[part, c0 : c0 + cw].astype(jnp.float32) + TY[part, c0 : c0 + cw].astype(jnp.float32)
             T[part, c0 : c0 + cw] = total.astype(jnp.bfloat16)
             return carry
 
@@ -515,7 +518,7 @@
     units = 12 * ROWS * WIDE // COLS
     total = W.at[pl.ds(0, units * (len(CHUNKS) + len(W_OVER_FIRST)))]
     all_b = remote(total, total, b_s, f_r, near[0])
-    total = G.at[pl.ds(0, units * (len(CHUNKS) + len(G_OVER_LAST)))]
+    total = W.at[pl.ds(0, units * (len(CHUNKS) + len(G_OVER_LAST)))]
     all_e = remote(total, total, e_s, f_r, near[0])
     sent.extend([all_f, all_b, all_e, remote(U, U, u_s, f_r, near[0])])
     drain()
@@ -549,9 +552,10 @@
             pltpu.VMEM((DW, 4 * TOK), bf16),
             pltpu.VMEM((4 * TOK, COLS), bf16),
             pltpu.VMEM((DW, COLS), bf16),
-            pltpu.VMEM((DW, COLS), bf16),
-            pltpu.VMEM((HALF, COLS), bf16),
-            pltpu.VMEM((3, 8 * ROWS, COLS), bf16),
+            pltpu.VMEM((2, 4, 4, ROWS, COLS), bf16),
+            pltpu.VMEM((4, 4, ROWS, COLS), bf16),
+            pltpu.VMEM((3, 8, ROWS, COLS), bf16),
+            pltpu.VMEM((4 * ROWS, COLS), bf16),
             pltpu.VMEM((4 * ROWS, COLS), bf16),
             pltpu.VMEM((4 * ROWS, COLS), bf16),
             pltpu.VMEM((4, ROWS, COLS), bf16),
@@ -573,7 +577,7 @@
             *sems,
         ],
         compiler_params=pltpu.CompilerParams(
-            collective_id=0, has_side_effects=True, vmem_limit_bytes=53 * 2**20
+            collective_id=0, has_side_effects=True, vmem_limit_bytes=int(52.75 * 2**20)
         ),
         cost_estimate=pl.CostEstimate(
             flops=4 * TOK * DW * FW, bytes_accessed=22 * 2**20, transcendentals=TOK * FW

time: 120 us -> 118 us (0.983)
  no operation moved by 1% of the time
where the time goes in v5:
time: 118 us
  Pallas kernels  114 us (97%)
  local copies, waits for them, and re-layouts  3.59 us (3%)
    pallas_call x1, Pallas kernels, local(): pl.pallas_call(kernel, name='inner_grad_outer_update', out_shape=(jax.Sha...  114 us
    unnamed x7, local copies, waits for them, and re-layouts  3.59 us

profile of v5, /device:TPU:0, one launch (start us, length us, event | category | flops | bytes accessed | tf_op | source)
XLA Modules:
  0.0 117.9 jit_solution(15475009500715645142)
XLA Ops:
  0.6 0.0 copy-start
  0.6 0.7 copy-done
  1.3 0.0 copy-start.1
  1.3 0.7 copy-done.1
  2.0 113.7 %inner_grad_outer_update.1 = (bf16[1,48,6144]{2,1,0:T(8,128)(2,1)S(1)}, f32[512,128]{1,0:T(8,128)S(1)}, f32[512,128]{1,0:T(8,128)S(1)}) custom-call(bf16[1,512,1536]{2,1,0:T(8,128)(2,1)} %x_hbm.1, s32[1,512]{1,0:T(1,128)S(1)} %copy-done, bf16[1,512,6144]{2,1,0:T(8,128)(2,1)} %up_hbm.1, bf16[1,48,6144]{2,1,0:T(8,128)(2,1)} %w_hbm.1, s32[16]{0:T(128)S(1)} %copy-done.1, ...), custom_call_target="tpu_custom_call" | custom-call | flops 19327352832 | bytes 23068672 | tf_op jit(solution)/shard_map/inner_grad_outer_update/pallas_call | solution.py:540
  115.7 0.8 copy.14
  116.5 0.7 copy.15
  117.2 0.7 copy.16
Async XLA Ops:
  0.6 0.7 copy-start
  1.3 0.7 copy-start.1
